TPU v7x, 32 devices: a whole 2x2x4 slice. The times are simulated.
32 devices in a mesh: row: 4 (over y, x), blk: 8 (over z, core).
Axes of the slice: x: 2, y: 2, z: 4, core: 2. Of those that a mesh axis runs over, the one named last changes fastest.
Arguments:
- tokens: bfloat16 [8, 512, 2048], P('row', 'blk'), may hold values from -6 to 6
- attn_weights: bfloat16 [2048, 8192], P(('row', 'blk')), may hold values from -0.1875 to 0.1875
- mlp_weights: bfloat16 [2048, 2, 8192], P(('row', 'blk')), may hold values from -0.125 to 0.125
- ln1_gain: float32 [2048], replicated, may hold values from 0.5 to 1.5
- ln1_bias: float32 [2048], replicated, may hold values from -1 to 1
- ln2_gain: float32 [2048], replicated, may hold values from 0.5 to 1.5
- ln2_bias: float32 [2048], replicated, may hold values from -1 to 1
- qkv_bias: float32 [6144], replicated, may hold values from -1 to 1
- dense_bias: float32 [2048], replicated, may hold values from -1 to 1
- up_bias: float32 [8192], replicated, may hold values from -2.5 to 2.5
- down_bias: float32 [2048], replicated, may hold values from -1 to 1
- doc_lengths: int32 [8, 4], P('row'), may hold values from 1 to 447, as said below
- cotangent: bfloat16 [8, 512, 2048], P('row', 'blk'), may hold values from -6 to 6
Outputs:
- layer_out: bfloat16 [8, 512, 2048], P('row', 'blk')
- tokens_grad: bfloat16 [8, 512, 2048], P('row', 'blk')
- attn_weights_grad: float32 [2048, 8192], P(('row', 'blk'))
- mlp_weights_grad: float32 [2048, 2, 8192], P(('row', 'blk'))
- ln1_gain_grad: float32 [2048], replicated
- ln1_bias_grad: float32 [2048], replicated
- ln2_gain_grad: float32 [2048], replicated
- ln2_bias_grad: float32 [2048], replicated
- qkv_bias_grad: float32 [6144], replicated
- dense_bias_grad: float32 [2048], replicated
- up_bias_grad: float32 [8192], replicated
- down_bias_grad: float32 [2048], replicated
Inputs may be any that keep to these rules, and one draw needn't show every extreme that they name: `doc_lengths`: each row's 4 lengths are whole numbers that sum to 512; in every group of 2 rows held by one index of row, one row holds a document of length 447 that starts within the first 64 positions and ends within the last 64 positions, and that row ends with a document of length 1.
All inputs are finite; a program needn't handle non-finite values.
Results may differ from a plain program's by a relative error of at most 0.013.
Values may be sent and summed in bfloat16 or wider, within the bound.
No kernel may reach another device: no remote copies, remote signals or barrier semaphores. Data moves between devices by JAX's collectives and lax.ppermute only.
A program may use at most 704 MiB of HBM per device.

v0:
```python
import functools
import math

import jax
import jax.numpy as jnp
import numpy as np
from jax import lax
from jax.experimental import pallas as pl
from jax.experimental.pallas import tpu as pltpu
from jax.sharding import PartitionSpec as P

HD = 256
ROT = 64
LANES = 128
BLOCK = 256
EPSILON = 1e-05
MASKED = -1e30
BF = jnp.bfloat16
F32 = jnp.float32
COST = 100
VMEM_LIMIT = 56 * 2**20
SMALL = 16 * 2**20


class Plan:
    def __init__(self, rows, blks, heads):
        self.rows = rows
        self.blks = blks
        self.share = blks // heads
        self.per_row = heads // rows
        self.group = blks // self.per_row
        self.groups = [
            list(range(i * self.group, (i + 1) * self.group)) for i in range(self.per_row)
        ]


def after(field, *others):
    return lax.optimization_barrier((field,) + others)[0] if others else field


def swap(field, axis, size, bit):
    return lax.ppermute(field, axis, [(i, i ^ bit) for i in range(size)])


def swap_group(field, plan, bits):
    return lax.ppermute(field, "blk", [(i, i ^ bits) for i in range(plan.blks)])


def gather_row(own, plan):
    return [own] + [swap(own, "row", plan.rows, k) for k in range(1, plan.rows)]


def scatter_row(pieces, plan, far=None):
    return [
        swap(v, "row", plan.rows, k)
        for k, v in enumerate(pieces)
        if k and (far is None or far == (k & (k - 1) != 0))
    ]


def dot(left, right, left_dim, right_dim):
    return lax.dot_general(
        left, right, (((left_dim,), (right_dim,)), ((), ())), preferred_element_type=F32
    )


def whole(array):
    return pl.BlockSpec(array.shape, lambda *i: (0,) * len(array.shape))


def like(shape, kind=BF):
    return jax.ShapeDtypeStruct(shape, kind)


def call(body, turns, grid, in_specs, out_specs, out_shape, operands, flops=0, limit=None):
    moved = sum(v.size * v.dtype.itemsize for v in operands)
    moved += sum(math.prod(v.shape) * jnp.dtype(v.dtype).itemsize for v in out_shape)
    return pl.pallas_call(
        body,
        name=getattr(body, "func", body).__name__,
        grid_spec=pltpu.PrefetchScalarGridSpec(
            num_scalar_prefetch=1, grid=(grid,), in_specs=in_specs, out_specs=out_specs
        ),
        out_shape=out_shape,
        compiler_params=pltpu.CompilerParams(vmem_limit_bytes=limit or VMEM_LIMIT),
        cost_estimate=pl.CostEstimate(
            flops=flops // COST, bytes_accessed=moved // COST, transcendentals=0
        ),
    )(turns, *operands)


def rows_block(columns, block=BLOCK):
    return pl.BlockSpec((block, columns), lambda i, t: (i, 0))


def add_kernel(t_ref, *refs):
    refs[-1][...] = sum(ref[...].astype(F32) for ref in refs[:-1]).astype(BF)


def add_pieces(turns, terms):
    depth, width = terms[0].shape
    block = rows_block(width, depth // 4)
    shape = like((depth, width))
    return call(
        add_kernel, turns, 4, [block] * len(terms), [block], [shape], terms, limit=SMALL
    )[0]


def turn_kernel(t_ref, x_ref, g_ref, v_ref, xo_ref, go_ref, vo_ref, s_ref):
    xo_ref[...] = x_ref[...]
    go_ref[...] = g_ref[...]
    vo_ref[...] = v_ref[...]
    s_ref[...] = jnp.sum(g_ref[...].astype(F32), 0, keepdims=True)


def turn_in(turns, x, g, vectors):
    rows = turns.shape[0]
    part = x.shape[1] // rows

    def specs(array, turned):
        index = (lambda k, t: (0, t[k])) if turned else (lambda k, t: (0, k))
        return pl.BlockSpec((array.shape[0], part), index)

    total_shape = like((1, x.shape[1]), F32)
    return call(
        turn_kernel,
        turns,
        rows,
        [specs(v, True) for v in (x, g, vectors)],
        [specs(v, False) for v in (x, g, vectors)] + [specs(total_shape, True)],
        [like(v.shape, v.dtype) for v in (x, g, vectors)] + [total_shape],
        [x, g, vectors],
    )


def split_kernel(t_ref, w_ref, u_ref, d_ref):
    u_ref[0] = w_ref[:, 0, :]
    d_ref[0] = w_ref[:, 1, :]


def split_mlp(turns, weights, blks):
    depth, _, hidden = weights.shape
    part = hidden // blks
    block = pl.BlockSpec((1, depth, part), lambda b, t: (b, 0, 0))
    return call(
        split_kernel,
        turns,
        blks,
        [pl.BlockSpec((depth, 2, part), lambda b, t: (0, 0, b))],
        [block] * 2,
        [like((blks, depth, part))] * 2,
        [weights],
    )


def join_kernel(t_ref, u_ref, d_ref, o_ref):
    o_ref[:, 0, :] = u_ref[0].astype(F32)
    o_ref[:, 1, :] = d_ref[0].astype(F32)


def join_mlp(turns, up, down):
    blks, depth, part = up.shape
    block = pl.BlockSpec((1, depth, part), lambda b, t: (b, 0, 0))
    return call(
        join_kernel,
        turns,
        blks,
        [block] * 2,
        [pl.BlockSpec((depth, 2, part), lambda b, t: (0, 0, b))],
        [like((depth, 2, blks * part), F32)],
        [up, down],
    )[0]


def split_attn_kernel(plan, width, t_ref, w_ref, qkv_ref, out_ref):
    b = pl.program_id(0)
    head = b % plan.group // plan.share * plan.per_row + b // plan.group
    for i in range(3):
        at = pl.multiple_of(i * width + head * HD, HD)
        qkv_ref[0, :, i * HD : (i + 1) * HD] = w_ref[:, pl.ds(at, HD)]

    @pl.when(b == 0)
    def _():
        out_ref[...] = w_ref[:, 3 * width :]


def split_attn(turns, weights, plan, width):
    depth = weights.shape[0]
    return call(
        functools.partial(split_attn_kernel, plan, width),
        turns,
        plan.blks,
        [whole(weights)],
        [
            pl.BlockSpec((1, depth, 3 * HD), lambda b, t: (b, 0, 0)),
            pl.BlockSpec((depth, width), lambda b, t: (0, 0)),
        ],
        [like((plan.blks, depth, 3 * HD)), like((depth, width))],
        [weights],
        limit=SMALL,
    )


def join_attn_kernel(plan, t_ref, qkv_ref, out_ref, o_ref):
    step = pl.program_id(0)
    heads = o_ref.shape[1] // HD

    @pl.when(step < 3)
    def _():
        at = pl.ds(pl.multiple_of(step * HD, HD), HD)
        for h in range(heads):
            first = h % plan.per_row * plan.group + h // plan.per_row * plan.share
            o_ref[:, h * HD : (h + 1) * HD] = sum(
                qkv_ref[first + i, :, at].astype(F32) for i in range(plan.share)
            )

    @pl.when(step == 3)
    def _():
        o_ref[...] = out_ref[...]


def join_attn(turns, qkv, out, plan):
    depth, width = out.shape
    return call(
        functools.partial(join_attn_kernel, plan),
        turns,
        4,
        [whole(qkv), whole(out)],
        [pl.BlockSpec((depth, width), lambda j, t: (0, j))],
        [like((depth, 4 * width), F32)],
        [qkv, out],
    )[0]


def pick_kernel(count, t_ref, *refs):
    pieces, outs = refs[:count], refs[count:]
    share = t_ref.shape[0] // len(outs)
    for n, out in enumerate(outs):
        for i in range(share):
            for k, piece in enumerate(pieces):

                @pl.when(t_ref[n * share + i] == k)
                def _(i=i, out=out, piece=piece):
                    out[...] = piece[...] if i == 0 else out[...] + piece[...]


def pick(table, pieces, count):
    return call(
        functools.partial(pick_kernel, len(pieces)),
        table,
        1,
        [whole(p) for p in pieces],
        [whole(pieces[0])] * count,
        [like(pieces[0].shape)] * count,
        pieces,
    )


def place_kernel(t_ref, *refs):
    *pieces, out_ref = refs
    for k, piece in enumerate(pieces):
        depth = piece.shape[0]
        out_ref[pl.ds(pl.multiple_of(t_ref[k] * depth, depth), depth)] = piece[...]


def place(table, pieces):
    depth, width = pieces[0].shape
    shape = like((len(pieces) * depth, width))
    return call(place_kernel, table, 1, [whole(p) for p in pieces], [whole(shape)], [shape], pieces)[0]


def norm_kernel(t_ref, x_ref, v_ref, a1_ref, a2_ref):
    field = x_ref[...].astype(F32)
    centred = field - jnp.mean(field, -1, keepdims=True)
    standard = centred * lax.rsqrt(jnp.mean(centred * centred, -1, keepdims=True) + EPSILON)
    a1_ref[...] = (standard * v_ref[0:1] + v_ref[1:2]).astype(BF)
    a2_ref[...] = (standard * v_ref[2:3] + v_ref[3:4]).astype(BF)


def norms(turns, x, vectors):
    count, width = x.shape
    return call(
        norm_kernel,
        turns,
        count // BLOCK,
        [rows_block(width), whole(vectors)],
        [rows_block(width)] * 2,
        [like(x.shape)] * 2,
        [x, vectors],
        20 * count * width,
    )


def times_pieces(left, pieces):
    out, start = None, 0
    for piece in pieces:
        depth = piece.shape[0]
        term = dot(left[:, start : start + depth], piece[...], 1, 0)
        out = term if out is None else out + term
        start += depth
    return out


def up_kernel(t_ref, a_ref, b_ref, *refs):
    pieces, (h_ref, s_ref) = refs[:-2], refs[-2:]
    pre = times_pieces(a_ref[...], pieces) + b_ref[...]
    cdf = 0.5 * (1.0 + lax.erf(pre * math.sqrt(0.5)))
    h_ref[...] = (pre * cdf).astype(BF)
    s_ref[...] = cdf + pre * (jnp.exp(-0.5 * pre * pre) * (1.0 / math.sqrt(2.0 * math.pi)))


def feed_up(turns, normed, bias, pieces):
    count, width = normed.shape
    hidden = bias.shape[0]
    return call(
        up_kernel,
        turns,
        count // BLOCK,
        [rows_block(width), pl.BlockSpec((1, hidden), lambda i, t: (0, 0))]
        + [whole(p) for p in pieces],
        [rows_block(hidden)] * 2,
        [like((count, hidden)), like((count, hidden), F32)],
        [normed, bias.reshape(1, hidden)] + pieces,
        2 * count * width * hidden,
    )


def slope_kernel(t_ref, g_ref, s_ref, *refs):
    pieces, (p_ref, sum_ref) = refs[:-2], refs[-2:]

    @pl.when(pl.program_id(0) == 0)
    def _():
        sum_ref[...] = jnp.zeros_like(sum_ref)

    grad = (times_pieces(g_ref[...], pieces) * s_ref[...]).astype(BF)
    p_ref[...] = grad
    sum_ref[...] += jnp.sum(grad.astype(F32), 0, keepdims=True)


def feed_slope(turns, grad, slope, pieces):
    count, width = grad.shape
    hidden = slope.shape[1]
    return call(
        slope_kernel,
        turns,
        count // BLOCK,
        [rows_block(width), rows_block(hidden)] + [whole(p) for p in pieces],
        [rows_block(hidden), pl.BlockSpec((1, hidden), lambda i, t: (0, 0))],
        [like((count, hidden)), like((1, hidden), F32)],
        [grad, slope] + pieces,
        2 * count * width * hidden,
    )


def lane_sum(field):
    return sum(field[:, i : i + LANES] for i in range(0, field.shape[1], LANES))


def weight_kernel(rows, with_sums, t_ref, l_ref, r_ref, *refs):
    step = pl.program_id(0)
    if with_sums:
        sum_ref, pieces, refs = refs[0], refs[1 : 1 + rows], refs[1 + rows :]
        parts_ref = refs[-1]
    grad = dot(l_ref[...], r_ref[...], 0, 0)
    for k in range(rows):

        @pl.when(step == k)
        def _(k=k):
            refs[k][...] = grad.astype(BF)
            if with_sums:
                piece = pieces[k][...].astype(F32)
                parts_ref[0] = lane_sum(piece * grad)
                parts_ref[1] = lane_sum(piece * sum_ref[...])


def weight_grad(turns, left, right, sums=None, pieces=()):
    rows = turns.shape[0]
    count, width = left.shape
    columns = right.shape[1]
    depth = width // rows
    out_shape = [like((depth, columns))] * rows
    out_specs = [whole(v) for v in out_shape]
    operands = [left, right]
    if pieces:
        operands += [sums] + pieces
        out_shape.append(like((2, width, LANES), F32))
        out_specs.append(pl.BlockSpec((2, depth, LANES), lambda k, t: (0, t[k], 0)))
    out = call(
        functools.partial(weight_kernel, rows, bool(pieces)),
        turns,
        rows,
        [pl.BlockSpec((count, depth), lambda k, t: (0, k))] + [whole(v) for v in operands[1:]],
        out_specs,
        out_shape,
        operands,
        2 * count * width * columns,
    )
    if pieces:
        return out[:-1], out[-1]
    return out


def out_kernel(rows, t_ref, o_ref, g_ref, *refs):
    *outs, grad_ref = refs
    depth = outs[0].shape[0]
    grad_ref[...] = dot(o_ref[...], g_ref[...], 0, 0)
    for j, out in enumerate(outs):
        at = pl.multiple_of(t_ref[rows + j] * depth, depth)
        out[...] = grad_ref[pl.ds(at, depth)].astype(BF)


def out_grad(turns, places, attended, grad):
    rows, group = turns.shape[0], places.shape[0]
    count, width = grad.shape
    part = width // rows
    depth = HD // group
    return pl.pallas_call(
        functools.partial(out_kernel, rows),
        name="out_kernel",
        grid_spec=pltpu.PrefetchScalarGridSpec(
            num_scalar_prefetch=1,
            grid=(rows,),
            in_specs=[whole(attended), pl.BlockSpec((count, part), lambda k, t: (0, k))],
            out_specs=[pl.BlockSpec((depth, part), lambda k, t: (0, t[k]))] * group,
            scratch_shapes=[pltpu.VMEM((HD, part), F32)],
        ),
        out_shape=[like((depth, width))] * group,
        compiler_params=pltpu.CompilerParams(vmem_limit_bytes=VMEM_LIMIT),
        cost_estimate=pl.CostEstimate(
            flops=2 * count * width * HD // COST,
            bytes_accessed=2 * (count * (width + HD) + width * HD) // COST,
            transcendentals=0,
        ),
    )(jnp.concatenate([turns, places]), attended, grad)


def turned_columns(t_ref, w_ref, k, depth):
    return w_ref[:, pl.ds(pl.multiple_of(t_ref[k] * depth, LANES), depth)]


def sum_kernel(t_ref, h_ref, o_ref, w_ref, *refs):
    pieces, y_ref = refs[:-1], refs[-1]
    for k, piece in enumerate(pieces):
        depth = piece.shape[0]
        term = dot(h_ref[...], piece[...], 1, 1)
        term += dot(o_ref[...], turned_columns(t_ref, w_ref, k, depth), 1, 0)
        y_ref[:, k * depth : (k + 1) * depth] = term.astype(BF)


def out_sum(turns, hidden, pieces, attended, out_w):
    count = hidden.shape[0]
    width = out_w.shape[1]
    return call(
        sum_kernel,
        turns,
        count // BLOCK,
        [rows_block(hidden.shape[1]), rows_block(HD), whole(out_w)] + [whole(p) for p in pieces],
        [rows_block(width)],
        [like((count, width))],
        [hidden, attended, out_w] + pieces,
        2 * count * width * (hidden.shape[1] + HD),
    )[0]


def back_kernel(t_ref, p_ref, q_ref, v_ref, *refs):
    pieces, c_ref = refs[:-1], refs[-1]
    count = len(pieces) // 2
    for k, (up, qkv) in enumerate(zip(pieces[:count], pieces[count:])):
        depth = up.shape[0]
        cols = slice(k * depth, (k + 1) * depth)
        term = dot(p_ref[...], up[...], 1, 1) * v_ref[2:3, cols]
        term += dot(q_ref[...], qkv[...], 1, 1) * v_ref[0:1, cols]
        c_ref[:, cols] = term.astype(BF)


def norm_back(turns, pre_grad, up_pieces, qkv_grad, qkv_pieces, vectors):
    count = pre_grad.shape[0]
    width = vectors.shape[1]
    columns = pre_grad.shape[1] + qkv_grad.shape[1]
    return call(
        back_kernel,
        turns,
        count // BLOCK,
        [rows_block(pre_grad.shape[1]), rows_block(qkv_grad.shape[1]), whole(vectors)]
        + [whole(p) for p in up_pieces + qkv_pieces],
        [rows_block(width)],
        [like((count, width))],
        [pre_grad, qkv_grad, vectors] + up_pieces + qkv_pieces,
        2 * count * width * columns,
    )[0]


def turned(field, cosine, minus, plus):
    head = field[:, :LANES]
    half = ROT // 2
    head = (
        head * cosine
        + pltpu.roll(head, LANES - half, 1) * minus
        + pltpu.roll(head, half, 1) * plus
    )
    return jnp.concatenate([head, field[:, LANES:]], 1)


def allowed_pairs(length, dq_ref, dk_ref):
    spot = lax.broadcasted_iota(jnp.int32, (length, length), 0)
    other = lax.broadcasted_iota(jnp.int32, (length, length), 1)
    return (dq_ref[0] == dk_ref[0]) & (other <= spot)


def forward_kernel(t_ref, a_ref, b_ref, c_ref, m_ref, p_ref, dq_ref, dk_ref, *refs):
    pieces, (qkv_ref, o_ref, lse_ref) = refs[:-3], refs[-3:]
    qkv = times_pieces(a_ref[...], pieces) + b_ref[...]
    tables = c_ref[0], m_ref[0], p_ref[0]
    queries = (turned(qkv[:, :HD], *tables) * HD ** (-0.5)).astype(BF)
    keys = turned(qkv[:, HD : 2 * HD], *tables).astype(BF)
    values = qkv[:, 2 * HD :].astype(BF)
    for i, field in enumerate((queries, keys, values)):
        qkv_ref[:, i * HD : (i + 1) * HD] = field
    allowed = allowed_pairs(a_ref.shape[0], dq_ref, dk_ref)
    scores = jnp.where(allowed, dot(queries, keys, 1, 1), MASKED)
    largest = jnp.max(scores, -1, keepdims=True)
    weights = jnp.where(allowed, jnp.exp(scores - largest), 0.0)
    mass = jnp.sum(weights, -1, keepdims=True)
    o_ref[...] = dot((weights / mass).astype(BF), values, 1, 0).astype(BF)
    lse_ref[...] = largest + jnp.log(mass)


def backward_kernel(
    parts, t_ref, g_ref, w_ref, qkv_ref, o_ref, lse_ref, c_ref, m_ref, p_ref, dq_ref, dk_ref,
    grad_ref, sum_ref,
):
    queries, keys, values = (qkv_ref[:, i * HD : (i + 1) * HD] for i in range(3))
    tables = c_ref[0], -m_ref[0], -p_ref[0]
    depth = w_ref.shape[1] // parts
    heads_grad = None
    for k in range(parts):
        cols = slice(k * depth, (k + 1) * depth)
        term = dot(g_ref[:, cols], turned_columns(t_ref, w_ref, k, depth), 1, 1)
        heads_grad = term if heads_grad is None else heads_grad + term
    heads_grad = heads_grad.astype(BF)
    allowed = allowed_pairs(g_ref.shape[0], dq_ref, dk_ref)
    scores = jnp.where(allowed, dot(queries, keys, 1, 1), MASKED)
    weights = jnp.where(allowed, jnp.exp(scores - lse_ref[...]), 0.0)
    deltas = jnp.sum(heads_grad.astype(F32) * o_ref[...].astype(F32), -1, keepdims=True)
    score_grad = (weights * (dot(heads_grad, values, 1, 1) - deltas)).astype(BF)
    query_grad = dot(score_grad, keys, 1, 0) * HD ** (-0.5)
    key_grad = dot(score_grad, queries, 0, 0)
    value_grad = dot(weights.astype(BF), heads_grad, 0, 0)
    fields = turned(query_grad, *tables), turned(key_grad, *tables), value_grad

    @pl.when(pl.program_id(0) == 0)
    def _():
        sum_ref[...] = jnp.zeros_like(sum_ref)

    for i, field in enumerate(fields):
        field = field.astype(BF)
        cols = slice(i * HD, (i + 1) * HD)
        grad_ref[:, cols] = field
        sum_ref[:, cols] += jnp.sum(field.astype(F32), 0, keepdims=True)


def pair_specs(length):
    table = pl.BlockSpec((1, length, LANES), lambda r, t: (r, 0, 0))
    return [table] * 3 + [
        pl.BlockSpec((1, length, 1), lambda r, t: (r, 0, 0)),
        pl.BlockSpec((1, 1, length), lambda r, t: (r, 0, 0)),
    ]


def head_forward(turns, normed, bias, pairs, pieces, length):
    count, width = normed.shape
    columns = 3 * HD
    return call(
        forward_kernel,
        turns,
        count // length,
        [rows_block(width, length), pl.BlockSpec((1, columns), lambda r, t: (0, 0))]
        + pair_specs(length)
        + [whole(p) for p in pieces],
        [rows_block(columns, length), rows_block(HD, length), rows_block(1, length)],
        [like((count, columns)), like((count, HD)), like((count, 1), F32)],
        [normed, bias.reshape(1, columns)] + pairs + pieces,
        2 * count * (width * columns + 2 * length * HD),
    )


def head_backward(turns, grad, out_w, qkv, attended, lse, pairs, length):
    count, width = grad.shape
    columns = 3 * HD
    return call(
        functools.partial(backward_kernel, turns.shape[0]),
        turns,
        count // length,
        [
            rows_block(width, length),
            whole(out_w),
            rows_block(columns, length),
            rows_block(HD, length),
            rows_block(1, length),
        ]
        + pair_specs(length),
        [rows_block(columns, length), pl.BlockSpec((1, columns), lambda r, t: (0, 0))],
        [like((count, columns)), like((1, columns), F32)],
        [grad, out_w, qkv, attended, lse] + pairs,
        2 * count * (width * HD + 5 * length * HD),
    )


def finish_kernel(rows, with_norm, t_ref, x_ref, s_ref, o_ref, out_ref):
    depth = x_ref.shape[1] // rows
    term = s_ref[...].astype(F32)
    if with_norm:
        centred = x_ref[...].astype(F32)
        centred = centred - jnp.mean(centred, -1, keepdims=True)
        rstd = lax.rsqrt(jnp.mean(centred * centred, -1, keepdims=True) + EPSILON)
        centred = centred * rstd
        term = term - jnp.mean(term, -1, keepdims=True) - centred * jnp.mean(
            term * centred, -1, keepdims=True
        )
        field = o_ref[...].astype(F32) + rstd * term
    else:
        field = x_ref[...].astype(F32) + term + o_ref[4:5]
    for k in range(rows):
        at = pl.multiple_of(t_ref[k] * depth, LANES)
        out_ref[:, pl.ds(at, depth)] = field[:, k * depth : (k + 1) * depth].astype(BF)


def finish(turns, x, term, other, with_norm):
    return call(
        functools.partial(finish_kernel, turns.shape[0], with_norm),
        turns,
        1,
        [whole(v) for v in (x, term, other)],
        [whole(x)],
        [like(x.shape)],
        [x, term, other],
    )[0]


def shards(
    plan,
    tokens,
    attn_weights,
    mlp_weights,
    ln1_gain,
    ln1_bias,
    ln2_gain,
    ln2_bias,
    qkv_bias,
    dense_bias,
    up_bias,
    down_bias,
    doc_lengths,
    cotangent,
):
    row_count, shard_len, width = tokens.shape
    depth = attn_weights.shape[0]
    heads = width // HD
    rows, blks = plan.rows, plan.blks
    own_hidden = mlp_weights.shape[-1] // blks
    me = lax.axis_index("blk")
    length = shard_len * blks
    count = row_count * length
    head_of = me % plan.group // plan.share * plan.per_row + me // plan.group
    part = me % plan.share
    own_rows = row_count // plan.share
    row = lax.axis_index("row")
    turns = row ^ jnp.arange(rows, dtype=jnp.int32)
    places = me % plan.group ^ jnp.arange(plan.group, dtype=jnp.int32)

    def exchange(field):
        return lax.all_to_all(field, "blk", 0, 0)

    def collect(field):
        return exchange(field.reshape(blks, -1, field.shape[-1]))

    def gather_blocks(field):
        field = field.reshape(row_count, shard_len, width)
        return lax.all_gather(field, "blk", axis=1, tiled=True).reshape(count, width)

    def sum_blocks(field):
        field = field.reshape(row_count, length, width)
        field = lax.psum_scatter(field, "blk", scatter_dimension=1, tiled=True)
        return field.reshape(row_count * shard_len, width)

    lengths = lax.dynamic_slice_in_dim(doc_lengths, part * own_rows, own_rows, 0)
    doc_ends = jnp.cumsum(lengths, axis=-1)
    starts = doc_ends - lengths
    spots = jnp.arange(length, dtype=jnp.int32)
    doc_ids = jnp.sum((spots[None, :, None] >= doc_ends[:, None, :]).astype(jnp.int32), -1)
    picked = doc_ids[:, :, None] == jnp.arange(lengths.shape[-1], dtype=jnp.int32)
    positions = spots - jnp.sum(jnp.where(picked, starts[:, None, :], 0), -1)
    lane = jnp.arange(LANES)
    inverse = 10000.0 ** (-2.0 * (lane % (ROT // 2)).astype(F32) / ROT)
    angles = positions.astype(F32)[..., None] * inverse
    sine = jnp.sin(angles)
    pairs = [
        jnp.where(lane < ROT, jnp.cos(angles), 1.0),
        jnp.where(lane < ROT // 2, -sine, 0.0),
        jnp.where((lane >= ROT // 2) & (lane < ROT), sine, 0.0),
        doc_ids[:, :, None],
        doc_ids[:, None, :],
    ]

    up_b = lax.dynamic_slice_in_dim(up_bias, me * own_hidden, own_hidden)
    qkv_b = lax.dynamic_index_in_dim(qkv_bias.reshape(3, heads, HD), head_of, 1, keepdims=False)
    qkv_b = qkv_b.reshape(-1)

    zeros = jnp.zeros((3, width), F32)
    vectors = jnp.stack([ln1_gain, ln1_bias, ln2_gain, ln2_bias, dense_bias + down_bias])
    x_own, g_own, vectors, g_sum = turn_in(
        turns,
        tokens.reshape(row_count * shard_len, width),
        cotangent.reshape(row_count * shard_len, width),
        jnp.concatenate([vectors, zeros]),
    )
    qkv_send, out_own = split_attn(turns, attn_weights, plan, width)
    qkv_mine = exchange(qkv_send)
    out_send = pick(
        row ^ places // plan.share,
        [out_own] + [swap(out_own, "row", rows, k) for k in range(1, rows)],
        plan.group,
    )
    up_send, down_send = split_mlp(turns, after(mlp_weights, qkv_send), blks)
    qkv_mine, up_send, *out_send = lax.optimization_barrier((qkv_mine, up_send, *out_send))
    up_mine = exchange(up_send)
    qkv_pieces = gather_row(qkv_mine.reshape(-1, 3 * HD), plan)
    out_got = [out_send[0]] + [swap_group(out_send[j], plan, j) for j in range(1, plan.group)]
    up_mine, x_own, down_send, *qkv_pieces = lax.optimization_barrier(
        (up_mine, x_own, down_send, *qkv_pieces, *out_got)
    )[: 3 + rows]
    x_all = gather_blocks(x_own)
    down_mine = exchange(down_send)
    up_pieces = gather_row(up_mine.reshape(-1, own_hidden), plan)
    out_w = place(places, out_got)
    down_mine, g_own, out_w, up_b, qkv_b, *pairs = lax.optimization_barrier(
        (down_mine, g_own, out_w, up_b, qkv_b, *pairs, *up_pieces)
    )
    pairs, up_pieces = pairs[: -len(up_pieces)], pairs[-len(up_pieces) :]
    g_all = gather_blocks(g_own)
    down_pieces = gather_row(down_mine.reshape(-1, own_hidden), plan)
    normed1, normed2 = norms(turns, x_all, vectors)

    def own(field):
        if plan.share == 1:
            return field
        return lax.dynamic_slice_in_dim(field, part * own_rows * length, own_rows * length, 0)

    def spread(field):
        if plan.share == 1:
            return field
        blank = jnp.zeros((count, field.shape[1]), field.dtype)
        return lax.dynamic_update_slice_in_dim(blank, field, part * own_rows * length, 0)

    own_normed1 = own(normed1)
    qkv, attended, lse = head_forward(
        turns, own_normed1, qkv_b, pairs, qkv_pieces, length
    )
    hidden, slope = feed_up(turns, after(normed2, attended), up_b, up_pieces)
    out_term = out_sum(turns, hidden, down_pieces, spread(attended), out_w)
    out_total = sum_blocks(out_term)

    g_all = after(g_all, out_term)
    down_g = weight_grad(turns, g_all, hidden)
    down_got = scatter_row(down_g, plan)
    own_grad = own(after(g_all, down_g[0]))
    out_g = out_grad(turns, places, attended, own_grad)
    out_got = [out_g[0]] + [swap_group(out_g[j], plan, j) for j in range(1, plan.group)]
    pre_grad, up_sum = feed_slope(turns, after(g_all, out_g[0]), slope, down_pieces)
    up_g, up_parts = weight_grad(turns, normed2, pre_grad, up_sum, up_pieces)
    qkv_grad, qkv_sum = head_backward(
        turns, after(own_grad, up_g[0]), out_w, qkv, attended, lse, pairs, length
    )
    down_total = add_pieces(turns, [after(down_g[0], qkv_grad, *out_got)] + down_got)
    down_back = collect(down_total)
    up_near = scatter_row([after(v, down_total) for v in up_g], plan, False)
    norm_term = norm_back(
        turns,
        after(pre_grad, down_total),
        up_pieces,
        spread(qkv_grad),
        qkv_pieces,
        vectors,
    )
    up_got = up_near + scatter_row([after(v, norm_term, *up_near) for v in up_g], plan, True)
    norm_total = sum_blocks(after(norm_term, down_back, *up_near))
    qkv_g, qkv_parts = weight_grad(
        turns,
        after(own_normed1, down_back, out_total, *up_near),
        qkv_grad,
        qkv_sum,
        qkv_pieces,
    )

    up_total = add_pieces(turns, [after(up_g[0], qkv_g[0])] + up_got)
    up_back = collect(up_total)
    qkv_got = scatter_row([after(v, up_total) for v in qkv_g], plan)

    terms = [jnp.sum(v, -1) for v in (qkv_parts, up_parts)]
    terms += [g_sum, qkv_sum, up_sum]
    terms = [v.reshape(-1) for v in terms]
    used = sum(v.size for v in terms)
    terms.append(jnp.zeros((-used % (8 * LANES),), F32))
    sums = jnp.concatenate(terms)
    sums = sums + sum(swap(sums, "row", rows, k) for k in range(1, rows))
    sums = after(sums, up_total)
    sums = jnp.stack([sums, swap(sums, "blk", blks, 1)])

    holders = turns[:, None] * plan.share + jnp.arange(plan.share, dtype=jnp.int32)
    holders = after((me % plan.group ^ holders).reshape(-1), sums)
    out_send = pick(holders, out_got, rows)
    layer_out = finish(turns, after(x_own, sums), out_total, vectors, False)

    joined = (up_back, layer_out, sums, out_send[0])
    qkv_total = add_pieces(turns, [after(qkv_g[0], *joined)] + qkv_got)
    qkv_back = collect(qkv_total)
    out_back = out_send[0].astype(F32) + sum(
        swap(after(out_send[k], qkv_total), "row", rows, k).astype(F32) for k in range(1, rows)
    )
    sums = after(sums, qkv_total)
    sums = jnp.concatenate([sums] + [swap(sums, "blk", blks, k) for k in range(2, blks, 2)])
    sums = sums[me ^ jnp.arange(blks, dtype=jnp.int32)]
    gain1, bias1, gain2, bias2, g_total = jnp.split(
        jnp.sum(sums[:, : 5 * width], 0), 5
    )
    sums = sums[:, 5 * width : used]
    qkv_bias_grad = sums[:, : 3 * HD].reshape(plan.per_row, rows, plan.share, 3, HD)
    qkv_bias_grad = jnp.sum(qkv_bias_grad, 2).transpose(2, 1, 0, 3).reshape(-1)
    up_bias_grad = sums[:, 3 * HD :].reshape(-1)

    tokens_grad = finish(turns, x_own, norm_total, g_own, True)
    return (
        layer_out.reshape(tokens.shape),
        tokens_grad.reshape(tokens.shape),
        join_attn(turns, qkv_back, after(out_back, tokens_grad), plan),
        join_mlp(turns, up_back, down_back),
        (gain1 - ln1_bias * bias1) / ln1_gain,
        bias1,
        (gain2 - ln2_bias * bias2) / ln2_gain,
        bias2,
        qkv_bias_grad,
        g_total,
        up_bias_grad,
        g_total,
    )


def solution(mesh):
    rows, blks = mesh.shape["row"], mesh.shape["blk"]
    vector = P()
    tokens = P("row", "blk", None)
    attn = P(("row", "blk"), None)
    mlp = P(("row", "blk"), None, None)

    def run(*arrays):
        plan = Plan(rows, blks, arrays[0].shape[-1] // HD)
        return jax.shard_map(
            functools.partial(shards, plan),
            mesh=mesh,
            in_specs=(tokens, attn, mlp) + (vector,) * 8 + (P("row", None), tokens),
            out_specs=(tokens, tokens, attn, mlp) + (vector,) * 8,
            check_vma=False,
        )(*arrays)

    return run
```

profile of v0, /device:TPU:0, one launch (start us, length us, event | category | flops | bytes accessed | tf_op | source)
XLA Modules:
  0.0 411.8 jit_solution(7541221858309212306)
XLA Ops:
  8.5 3.2 split_attn_kernel.1
  11.7 6.3 %all-to-all-start = ((bf16[8,64,768]{2,1,0:T(8,128)(2,1)}), bf16[8,64,768]{2,1,0:T(8,128)(2,1)S(1)}, u32[]{:S(2)}, u32[]{:S(2)}) async-start(bf16[8,64,768]{2,1,0:T(8,128)(2,1)} %get-tuple-element.110), calls=%async_computation | async-start | bytes 1572864 | tf_op jit(solution)/shard_map/all_to_all | solution.py:672
  18.0 2.4 collective-permute-start.2
  21.5 8.4 %split_kernel.1 = (bf16[8,64,1024]{2,1,0:T(8,128)(2,1)}, bf16[8,64,1024]{2,1,0:T(8,128)(2,1)}) custom-call(s32[4]{0:T(128)} %copy-done.5, bf16[64,2,8192]{2,1,0:T(2,128)(2,1)} %w_ref.2), custom_call_target="tpu_custom_call" | custom-call | bytes 41943 | tf_op jit(solution)/shard_map/split_kernel/pallas_call | solution.py:78
  30.5 2.8 collective-permute-done.1.refs_2_
  34.6 3.0 pick_kernel.2
  39.0 3.6 all-to-all-start.1
  42.6 2.5 collective-permute-start.5
  50.4 4.2 %turn_kernel.1 = (bf16[128,2048]{1,0:T(8,128)(2,1)}, bf16[128,2048]{1,0:T(8,128)(2,1)}, f32[8,2048]{1,0:T(8,128)}, f32[1,2048]{1,0:T(1,128)}) custom-call(s32[4]{0:T(128)} %copy-done.5, bf16[128,2048]{1,0:T(8,128)(2,1)} %bitcast.71, bf16[128,2048]{1,0:T(8,128)(2,1)} %bitcast.72, f32[8,2048]{1,0:T(8,128)} %concatenate.12.v_ref), custom_call_target="tpu_custom_call" | custom-call | bytes 22364 | tf_op jit(solution)/shard_map/turn_kernel/pallas_call | solution.py:78
  54.6 11.9 %collective-permute-done.7.refs_2_ = bf16[64,2048]{1,0:T(8,128)(2,1)} collective-permute-done((bf16[64,2048]{1,0:T(8,128)(2,1)}, bf16[64,2048]{1,0:T(8,128)(2,1)}, u32[]{:S(2)}, u32[]{:S(2)}) %collective-permute-start.7) | collective-permute-done | bytes 262176 | tf_op jit(solution)/shard_map/ppermute | solution.py:46
  66.5 7.0 %collective-permute-done.8.refs_3_ = bf16[64,2048]{1,0:T(8,128)(2,1)} collective-permute-done((bf16[64,2048]{1,0:T(8,128)(2,1)}, bf16[64,2048]{1,0:T(8,128)(2,1)}, u32[]{:S(2)}, u32[]{:S(2)}) %collective-permute-start.8) | collective-permute-done | bytes 262176 | tf_op jit(solution)/shard_map/ppermute | solution.py:46
  73.4 6.8 %collective-permute-done.4.refs_2_.refs_3_.refs_6_ = bf16[512,768]{1,0:T(8,128)(2,1)S(1)} collective-permute-done((bf16[512,768]{1,0:T(8,128)(2,1)S(1)}, bf16[512,768]{1,0:T(8,128)(2,1)S(1)}, u32[]{:S(2)}, u32[]{:S(2)}) %collective-permute-start.4) | collective-permute-done | bytes 786464 | tf_op jit(solution)/shard_map/ppermute | solution.py:42
  81.1 4.8 %all-to-all-start.2 = ((bf16[8,64,1024]{2,1,0:T(8,128)(2,1)}), bf16[8,64,1024]{2,1,0:T(8,128)(2,1)S(1)}, u32[]{:S(2)}, u32[]{:S(2)}) async-start(bf16[8,64,1024]{2,1,0:T(8,128)(2,1)} %get-tuple-element.129), calls=%async_computation.2 | async-start | bytes 2097152 | tf_op jit(solution)/shard_map/all_to_all | solution.py:672
  92.3 3.2 fusion
  95.5 2.9 place_kernel.1.w_ref
  98.4 16.7 %collective-permute-done.11.refs_3_.refs_4_ = bf16[512,1024]{1,0:T(8,128)(2,1)S(1)} collective-permute-done((bf16[512,1024]{1,0:T(8,128)(2,1)S(1)}, bf16[512,1024]{1,0:T(8,128)(2,1)S(1)}, u32[]{:S(2)}, u32[]{:S(2)}) %collective-permute-start.11) | collective-permute-done | bytes 1048608 | tf_op jit(solution)/shard_map/ppermute | solution.py:42
  115.1 22.0 %collective-permute-done.10.refs_2_.refs_3_ = bf16[512,1024]{1,0:T(8,128)(2,1)S(1)} collective-permute-done((bf16[512,1024]{1,0:T(8,128)(2,1)S(1)}, bf16[512,1024]{1,0:T(8,128)(2,1)S(1)}, u32[]{:S(2)}, u32[]{:S(2)}) %collective-permute-start.10) | collective-permute-done | bytes 1048608 | tf_op jit(solution)/shard_map/ppermute | solution.py:42
  143.6 4.3 %all-gather.3.cloned.1.call-done = bf16[2,512,2048]{2,1,0:T(8,128)(2,1)} async-done(((bf16[2,64,2048]{2,1,0:T(8,128)(2,1)}), bf16[2,512,2048]{2,1,0:T(8,128)(2,1)}) %all-gather.3.cloned.1.call-update) | async-done | bytes 4194320 | tf_op jit(solution)/shard_map/all_gather | solution.py:679
  147.9 8.5 %norm_kernel.1 = (bf16[1024,2048]{1,0:T(8,128)(2,1)}, bf16[1024,2048]{1,0:T(8,128)(2,1)}) custom-call(s32[4]{0:T(128)} %copy-done.5, bf16[1024,2048]{1,0:T(8,128)(2,1)} %bitcast.67, f32[8,2048]{1,0:T(8,128)} %get-tuple-element.127.v_ref.o_ref), custom_call_target="tpu_custom_call" | custom-call | flops 419430 | bytes 126484 | tf_op jit(solution)/shard_map/norm_kernel/pallas_call | solution.py:78
  156.4 9.8 %forward_kernel.1 = (bf16[1024,768]{1,0:T(8,128)(2,1)}, bf16[1024,256]{1,0:T(8,128)(2,1)}, f32[1024,1]{1,0:T(8,128)}) custom-call(s32[4]{0:T(128)} %copy-done.5, bf16[1024,2048]{1,0:T(8,128)(2,1)} %get-tuple-element.178.a_ref.l_ref, f32[1,768]{1,0:T(1,128)} %reshape.168.b_ref, f32[2,512,128]{2,1,0:T(8,128)} %get-tuple-element.135.c_ref, ...), custom_call_target="tpu_custom_call" | custom-call | flops 37580964 | bytes 110254 | tf_op jit(solution)/shard_map/forward_kernel/pallas_call | solution.py:78
  166.1 10.9 %up_kernel.1 = (bf16[1024,1024]{1,0:T(8,128)(2,1)}, f32[1024,1024]{1,0:T(8,128)}) custom-call(s32[4]{0:T(128)} %copy-done.5, bf16[1024,2048]{1,0:T(8,128)(2,1)} %get-tuple-element.145.a_ref.l_ref, f32[1,1024]{1,0:T(1,128)} %bitcast.92, bf16[512,1024]{1,0:T(8,128)(2,1)} %bitcast.52, bf16[512,1024]{1,0:T(8,128)(2,1)} %collective-permute-done.9.refs_1_.refs_2_, ...), custom_call_target="tpu_custom_call" | custom-call | flops 42949672 | bytes 146841 | tf_op jit(solution)/shard_map/up_kernel/pallas_call | solution.py:78
  177.0 10.0 %collective-permute-done.13.refs_2_ = bf16[512,1024]{1,0:T(8,128)(2,1)} collective-permute-done((bf16[512,1024]{1,0:T(8,128)(2,1)S(1)}, bf16[512,1024]{1,0:T(8,128)(2,1)}, u32[]{:S(2)}, u32[]{:S(2)}) %collective-permute-start.13) | collective-permute-done | bytes 1048608 | tf_op jit(solution)/shard_map/ppermute | solution.py:42
  187.2 10.6 %sum_kernel.1 = bf16[1024,2048]{1,0:T(8,128)(2,1)} custom-call(s32[4]{0:T(128)} %copy-done.5, bf16[1024,1024]{1,0:T(8,128)(2,1)} %get-tuple-element.151.h_ref.r_ref, bf16[1024,256]{1,0:T(8,128)(2,1)} %get-tuple-element.144.o_ref, bf16[256,2048]{1,0:T(8,128)(2,1)} %place_kernel.1.w_ref, bf16[512,1024]{1,0:T(8,128)(2,1)} %bitcast.64, ...), custom_call_target="tpu_custom_call" | custom-call | flops 53687092 | bytes 120586 | tf_op jit(solution)/shard_map/sum_kernel/pallas_call | solution.py:78
  197.9 10.3 %weight_kernel.3 = (bf16[512,1024]{1,0:T(8,128)(2,1)}, bf16[512,1024]{1,0:T(8,128)(2,1)}, bf16[512,1024]{1,0:T(8,128)(2,1)}, bf16[512,1024]{1,0:T(8,128)(2,1)}) custom-call(s32[4]{0:T(128)} %copy-done.5, bf16[1024,2048]{1,0:T(8,128)(2,1)} %bitcast.43, bf16[1024,1024]{1,0:T(8,128)(2,1)} %get-tuple-element.151.h_ref.r_ref), custom_call_target="tpu_custom_call" | custom-call | flops 42949672 | bytes 104857 | tf_op jit(solution)/shard_map/weight_kernel/pallas_call | solution.py:78
  212.2 5.8 %out_kernel.1 = (bf16[64,2048]{1,0:T(8,128)(2,1)}, bf16[64,2048]{1,0:T(8,128)(2,1)}, bf16[64,2048]{1,0:T(8,128)(2,1)}, bf16[64,2048]{1,0:T(8,128)(2,1)}) custom-call(s32[8]{0:T(128)} %pad_add_fusion.t_ref, bf16[1024,256]{1,0:T(8,128)(2,1)} %get-tuple-element.144.o_ref, bf16[1024,2048]{1,0:T(8,128)(2,1)} %bitcast.44), custom_call_target="tpu_custom_call" | custom-call | flops 10737418 | bytes 57671 | tf_op jit(solution)/shard_map/out_kernel/pallas_call | solution.py:417
  220.9 10.0 %slope_kernel.1 = (bf16[1024,1024]{1,0:T(8,128)(2,1)}, f32[1,1024]{1,0:T(1,128)}) custom-call(s32[4]{0:T(128)} %copy-done.5, bf16[1024,2048]{1,0:T(8,128)(2,1)} %bitcast.45, f32[1024,1024]{1,0:T(8,128)} %get-tuple-element.159.s_ref, bf16[512,1024]{1,0:T(8,128)(2,1)} %bitcast.65, bf16[512,1024]{1,0:T(8,128)(2,1)} %collective-permute-done.12.refs_1_, ...), custom_call_target="tpu_custom_call" | custom-call | flops 42949672 | bytes 146841 | tf_op jit(solution)/shard_map/slope_kernel/pallas_call | solution.py:78
  231.0 13.4 %weight_kernel.4 = (bf16[512,1024]{1,0:T(8,128)(2,1)}, bf16[512,1024]{1,0:T(8,128)(2,1)}, bf16[512,1024]{1,0:T(8,128)(2,1)}, bf16[512,1024]{1,0:T(8,128)(2,1)}, f32[2,2048,128]{2,1,0:T(8,128)}) custom-call(s32[4]{0:T(128)} %copy-done.5, bf16[1024,2048]{1,0:T(8,128)(2,1)} %get-tuple-element.145.a_ref.l_ref, ...), custom_call_target="tpu_custom_call" | custom-call | flops 42949672 | bytes 167813 | tf_op jit(solution)/shard_map/weight_kernel/pallas_call | solution.py:78
  244.3 10.2 %backward_kernel.1 = (bf16[1024,768]{1,0:T(8,128)(2,1)}, f32[1,768]{1,0:T(1,128)}) custom-call(s32[4]{0:T(128)} %copy-done.5, bf16[1024,2048]{1,0:T(8,128)(2,1)} %bitcast.46, bf16[256,2048]{1,0:T(8,128)(2,1)} %place_kernel.1.w_ref, bf16[1024,768]{1,0:T(8,128)(2,1)} %get-tuple-element.164.qkv_ref, bf16[1024,256]{1,0:T(8,128)(2,1)} %get-tuple-element.144.o_ref, ...), custom_call_target="tpu_custom_call" | custom-call | flops 24159192 | bytes 105011 | tf_op jit(solution)/shard_map/backward_kernel/pallas_call | solution.py:78
  254.6 2.4 collective-permute-done.19.refs_2_
  257.0 2.4 add_kernel.3
  259.3 4.6 %all-to-all-start.3 = ((bf16[8,64,1024]{2,1,0:T(8,128)(2,1)}), bf16[8,64,1024]{2,1,0:T(8,128)(2,1)S(1)}, u32[]{:S(2)}, u32[]{:S(2)}) async-start(bf16[8,64,1024]{2,1,0:T(8,128)(2,1)} %bitcast.16), calls=%async_computation.3 | async-start | bytes 2097152 | tf_op jit(solution)/shard_map/all_to_all | solution.py:672
  266.2 13.7 %back_kernel.1 = bf16[1024,2048]{1,0:T(8,128)(2,1)} custom-call(s32[4]{0:T(128)} %copy-done.5, bf16[1024,1024]{1,0:T(8,128)(2,1)} %get-tuple-element.186.r_ref.p_ref, bf16[1024,768]{1,0:T(8,128)(2,1)} %get-tuple-element.166.r_ref.q_ref, f32[8,2048]{1,0:T(8,128)} %get-tuple-element.127.v_ref.o_ref, bf16[512,1024]{1,0:T(8,128)(2,1)} %bitcast.54, ...), custom_call_target="tpu_custom_call" | custom-call | flops 75161928 | bytes 152698 | tf_op jit(solution)/shard_map/back_kernel/pallas_call | solution.py:78
  279.9 9.8 %collective-permute-done.21.refs_1_ = bf16[512,1024]{1,0:T(8,128)(2,1)S(1)} collective-permute-done((bf16[512,1024]{1,0:T(8,128)(2,1)}, bf16[512,1024]{1,0:T(8,128)(2,1)S(1)}, u32[]{:S(2)}, u32[]{:S(2)}) %collective-permute-start.21) | collective-permute-done | bytes 1048608 | tf_op jit(solution)/shard_map/ppermute | solution.py:42
  294.5 11.5 %weight_kernel.5 = (bf16[512,768]{1,0:T(8,128)(2,1)}, bf16[512,768]{1,0:T(8,128)(2,1)}, bf16[512,768]{1,0:T(8,128)(2,1)}, bf16[512,768]{1,0:T(8,128)(2,1)}, f32[2,2048,128]{2,1,0:T(8,128)}) custom-call(s32[4]{0:T(128)} %copy-done.5, bf16[1024,2048]{1,0:T(8,128)(2,1)} %get-tuple-element.178.a_ref.l_ref, bf16[1024,768]{1,0:T(8,128)(2,1)} %get-tuple-element.166.r_ref.q_ref, ...), custom_call_target="tpu_custom_call" | custom-call | flops 32212254 | bytes 141588 | tf_op jit(solution)/shard_map/weight_kernel/pallas_call | solution.py:78
  311.9 5.7 %collective-permute-done.26.refs_3_ = bf16[512,1024]{1,0:T(8,128)(2,1)} collective-permute-done((bf16[512,1024]{1,0:T(8,128)(2,1)}, bf16[512,1024]{1,0:T(8,128)(2,1)}, u32[]{:S(2)}, u32[]{:S(2)}) %collective-permute-start.26) | collective-permute-done | bytes 1048608 | tf_op jit(solution)/shard_map/ppermute | solution.py:42
  317.7 4.1 %add_kernel.4 = bf16[512,1024]{1,0:T(8,128)(2,1)} custom-call(s32[4]{0:T(128)S(1)} %copy-done.8, bf16[512,1024]{1,0:T(8,128)(2,1)S(1)} %copy-done.1, bf16[512,1024]{1,0:T(8,128)(2,1)S(1)} %collective-permute-done.21.refs_1_, bf16[512,1024]{1,0:T(8,128)(2,1)S(1)} %collective-permute-done.22.refs_2_, bf16[512,1024]{1,0:T(8,128)(2,1)} %collective-permute-done.26.refs_3_), custom_call_target="tpu_custom_call" | custom-call | bytes 52428 | tf_op jit(solution)/shard_map/add_kernel/pallas_call | solution.py:78
  321.8 4.3 %all-to-all-start.4 = ((bf16[8,64,1024]{2,1,0:T(8,128)(2,1)}), bf16[8,64,1024]{2,1,0:T(8,128)(2,1)}, u32[]{:S(2)}, u32[]{:S(2)}) async-start(bf16[8,64,1024]{2,1,0:T(8,128)(2,1)} %bitcast.27), calls=%async_computation.6 | async-start | bytes 2097152 | tf_op jit(solution)/shard_map/all_to_all | solution.py:672
  330.7 2.9 finish_kernel.2
  333.5 3.0 pick_kernel.3
  336.5 25.4 %all-to-all-done.4.u_ref = bf16[8,64,1024]{2,1,0:T(8,128)(2,1)} async-done(((bf16[8,64,1024]{2,1,0:T(8,128)(2,1)}), bf16[8,64,1024]{2,1,0:T(8,128)(2,1)}, u32[]{:S(2)}, u32[]{:S(2)}) %all-to-all-start.4) | async-done | bytes 1048608 | tf_op jit(solution)/shard_map/all_to_all | solution.py:672
  361.9 2.3 collective-permute-done.29.refs_2_
  365.4 2.2 add_kernel.5
  367.6 3.8 collective-permute-start.36
  372.0 5.1 %all-to-all-start.5 = ((bf16[8,64,768]{2,1,0:T(8,128)(2,1)}), bf16[8,64,768]{2,1,0:T(8,128)(2,1)S(1)}, u32[]{:S(2)}, u32[]{:S(2)}) async-start(bf16[8,64,768]{2,1,0:T(8,128)(2,1)} %bitcast.28), calls=%async_computation.7 | async-start | bytes 1572864 | tf_op jit(solution)/shard_map/all_to_all | solution.py:672
  379.3 7.1 %join_kernel.1 = f32[64,2,8192]{2,1,0:T(2,128)} custom-call(s32[4]{0:T(128)} %copy-done.5, bf16[8,64,1024]{2,1,0:T(8,128)(2,1)} %all-to-all-done.4.u_ref, bf16[8,64,1024]{2,1,0:T(8,128)(2,1)} %copy-done.17), custom_call_target="tpu_custom_call" | custom-call | bytes 62914 | tf_op jit(solution)/shard_map/join_kernel/pallas_call | solution.py:78
  390.8 4.7 %collective-permute-done.33 = bf16[64,2048]{1,0:T(8,128)(2,1)S(1)} collective-permute-done((bf16[64,2048]{1,0:T(8,128)(2,1)S(1)}, bf16[64,2048]{1,0:T(8,128)(2,1)S(1)}, u32[]{:S(2)}, u32[]{:S(2)}) %collective-permute-start.33) | collective-permute-done | bytes 262176 | tf_op jit(solution)/shard_map/ppermute | solution.py:42
  396.5 3.5 finish_kernel.3
  400.9 3.8 join_attn_kernel.1
  (207 shorter events, 59.8 us)
Async XLA Ops:
  11.7 27.3 %all-to-all-start = ((bf16[8,64,768]{2,1,0:T(8,128)(2,1)}), bf16[8,64,768]{2,1,0:T(8,128)(2,1)S(1)}, u32[]{:S(2)}, u32[]{:S(2)}) async-start(bf16[8,64,768]{2,1,0:T(8,128)(2,1)} %get-tuple-element.110), calls=%async_computation | async-start | bytes 1572864 | tf_op jit(solution)/shard_map/all_to_all | solution.py:672
  18.0 12.4 %collective-permute-start.2 = (bf16[64,2048]{1,0:T(8,128)(2,1)S(1)}, bf16[64,2048]{1,0:T(8,128)(2,1)S(1)}, u32[]{:S(2)}, u32[]{:S(2)}) collective-permute-start(bf16[64,2048]{1,0:T(8,128)(2,1)S(1)} %get-tuple-element.113.refs_0_), channel_id=1, source_target_pairs={{0,24},{8,16},{16,8},{24,0},{1,25},{9,17},{17,9},{25,1},{2,26},{10... | collective-permute-start | bytes 786440 | tf_op jit(solution)/shard_map/ppermute | solution.py:42
  20.5 12.8 %collective-permute-start.1 = (bf16[64,2048]{1,0:T(8,128)(2,1)S(1)}, bf16[64,2048]{1,0:T(8,128)(2,1)S(1)}, u32[]{:S(2)}, u32[]{:S(2)}) collective-permute-start(bf16[64,2048]{1,0:T(8,128)(2,1)S(1)} %get-tuple-element.113.refs_0_), channel_id=1, source_target_pairs={{0,16},{8,24},{16,0},{24,8},{1,17},{9,25},{17,1},{25,9},{2,18},{10... | collective-permute-start | bytes 786440 | tf_op jit(solution)/shard_map/ppermute | solution.py:42
  21.0 12.4 %collective-permute-start = (bf16[64,2048]{1,0:T(8,128)(2,1)S(1)}, bf16[64,2048]{1,0:T(8,128)(2,1)S(1)}, u32[]{:S(2)}, u32[]{:S(2)}) collective-permute-start(bf16[64,2048]{1,0:T(8,128)(2,1)S(1)} %get-tuple-element.113.refs_0_), channel_id=1, source_target_pairs={{0,8},{8,0},{16,24},{24,16},{1,9},{9,1},{17,25},{25,17},{2,10},{10... | collective-permute-start | bytes 786440 | tf_op jit(solution)/shard_map/ppermute | solution.py:42
  39.0 41.4 %all-to-all-start.1 = ((bf16[8,64,1024]{2,1,0:T(8,128)(2,1)}), bf16[8,64,1024]{2,1,0:T(8,128)(2,1)S(1)}, u32[]{:S(2)}, u32[]{:S(2)}) async-start(bf16[8,64,1024]{2,1,0:T(8,128)(2,1)} %get-tuple-element.118), calls=%async_computation.1 | async-start | bytes 2097152 | tf_op jit(solution)/shard_map/all_to_all | solution.py:672
  42.6 105.3 %all-gather.3.cloned.1.call-start = ((), (), s32[]{:S(2)}) async-start(), calls=%async_computation.8 | async-start | bytes 4718592 | tf_op jit(solution)/shard_map/all_gather | solution.py:679
  42.6 30.8 %collective-permute-start.5 = (bf16[512,768]{1,0:T(8,128)(2,1)S(1)}, bf16[512,768]{1,0:T(8,128)(2,1)S(1)}, u32[]{:S(2)}, u32[]{:S(2)}) collective-permute-start(bf16[512,768]{1,0:T(8,128)(2,1)S(1)} %bitcast.55), channel_id=1, source_target_pairs={{0,24},{8,16},{16,8},{24,0},{1,25},{9,17},{17,9},{25,1},{2,26},{10... | collective-permute-start | bytes 2359304 | tf_op jit(solution)/shard_map/ppermute | solution.py:42
  45.1 35.0 %collective-permute-start.4 = (bf16[512,768]{1,0:T(8,128)(2,1)S(1)}, bf16[512,768]{1,0:T(8,128)(2,1)S(1)}, u32[]{:S(2)}, u32[]{:S(2)}) collective-permute-start(bf16[512,768]{1,0:T(8,128)(2,1)S(1)} %bitcast.56), channel_id=1, source_target_pairs={{0,16},{8,24},{16,0},{24,8},{1,17},{9,25},{17,1},{25,9},{2,18},{10... | collective-permute-start | bytes 2359304 | tf_op jit(solution)/shard_map/ppermute | solution.py:42
  45.6 34.7 %collective-permute-start.3 = (bf16[512,768]{1,0:T(8,128)(2,1)S(1)}, bf16[512,768]{1,0:T(8,128)(2,1)}, u32[]{:S(2)}, u32[]{:S(2)}) collective-permute-start(bf16[512,768]{1,0:T(8,128)(2,1)S(1)} %bitcast.57), channel_id=1, source_target_pairs={{0,8},{8,0},{16,24},{24,16},{1,9},{9,1},{17,25},{25,17},{2,10},{10... | collective-permute-start | bytes 2359304 | tf_op jit(solution)/shard_map/ppermute | solution.py:42
  46.2 1.9 collective-permute-start.6
  46.2 20.3 %collective-permute-start.7 = (bf16[64,2048]{1,0:T(8,128)(2,1)}, bf16[64,2048]{1,0:T(8,128)(2,1)}, u32[]{:S(2)}, u32[]{:S(2)}) collective-permute-start(bf16[64,2048]{1,0:T(8,128)(2,1)} %get-tuple-element.124), channel_id=1, source_target_pairs={{0,2},{1,3},{2,0},{3,1},{4,6},{5,7},{6,4},{7,5},{8,10},{9,11},{10,... | collective-permute-start | bytes 786440 | tf_op jit(solution)/shard_map/ppermute | solution.py:46
  48.0 25.4 %collective-permute-start.8 = (bf16[64,2048]{1,0:T(8,128)(2,1)}, bf16[64,2048]{1,0:T(8,128)(2,1)}, u32[]{:S(2)}, u32[]{:S(2)}) collective-permute-start(bf16[64,2048]{1,0:T(8,128)(2,1)} %get-tuple-element.125), channel_id=1, source_target_pairs={{0,3},{1,2},{2,1},{3,0},{4,7},{5,6},{6,5},{7,4},{8,11},{9,10},{10,... | collective-permute-start | bytes 786440 | tf_op jit(solution)/shard_map/ppermute | solution.py:46
  80.4 76.0 %copy-start.10 = (bf16[8,64,1024]{2,1,0:T(8,128)(2,1)}, bf16[8,64,1024]{2,1,0:T(8,128)(2,1)S(1)}, u32[]{:S(2)}) copy-start(bf16[8,64,1024]{2,1,0:T(8,128)(2,1)S(1)} %all-to-all-done.1) | copy-start | bytes 3145732
  81.1 57.1 %all-to-all-start.2 = ((bf16[8,64,1024]{2,1,0:T(8,128)(2,1)}), bf16[8,64,1024]{2,1,0:T(8,128)(2,1)S(1)}, u32[]{:S(2)}, u32[]{:S(2)}) async-start(bf16[8,64,1024]{2,1,0:T(8,128)(2,1)} %get-tuple-element.129), calls=%async_computation.2 | async-start | bytes 2097152 | tf_op jit(solution)/shard_map/all_to_all | solution.py:672
  85.9 112.0 %all-gather.5.cloned.1.call-start = ((), (), s32[]{:S(2)}) async-start(), calls=%async_computation.9 | async-start | bytes 4718592 | tf_op jit(solution)/shard_map/all_gather | solution.py:679
  88.2 26.9 %collective-permute-start.11 = (bf16[512,1024]{1,0:T(8,128)(2,1)S(1)}, bf16[512,1024]{1,0:T(8,128)(2,1)S(1)}, u32[]{:S(2)}, u32[]{:S(2)}) collective-permute-start(bf16[512,1024]{1,0:T(8,128)(2,1)S(1)} %bitcast.49), channel_id=1, source_target_pairs={{0,24},{8,16},{16,8},{24,0},{1,25},{9,17},{17,9},{25,1},{2,26},{10... | collective-permute-start | bytes 3145736 | tf_op jit(solution)/shard_map/ppermute | solution.py:42
  89.9 47.1 %collective-permute-start.10 = (bf16[512,1024]{1,0:T(8,128)(2,1)S(1)}, bf16[512,1024]{1,0:T(8,128)(2,1)S(1)}, u32[]{:S(2)}, u32[]{:S(2)}) collective-permute-start(bf16[512,1024]{1,0:T(8,128)(2,1)S(1)} %bitcast.50), channel_id=1, source_target_pairs={{0,16},{8,24},{16,0},{24,8},{1,17},{9,25},{17,1},{25,9},{2,18},{10... | collective-permute-start | bytes 3145736 | tf_op jit(solution)/shard_map/ppermute | solution.py:42
  91.1 46.9 %collective-permute-start.9 = (bf16[512,1024]{1,0:T(8,128)(2,1)S(1)}, bf16[512,1024]{1,0:T(8,128)(2,1)}, u32[]{:S(2)}, u32[]{:S(2)}) collective-permute-start(bf16[512,1024]{1,0:T(8,128)(2,1)S(1)} %bitcast.51), channel_id=1, source_target_pairs={{0,8},{8,0},{16,24},{24,16},{1,9},{9,1},{17,25},{25,17},{2,10},{10... | collective-permute-start | bytes 3145736 | tf_op jit(solution)/shard_map/ppermute | solution.py:42
  138.2 156.3 %reduce-scatter.3.cloned.1.call-start = ((), (), s32[]{:S(2)}) async-start(), calls=%async_computation.10 | async-start | bytes 4718592 | tf_op jit(solution)/shard_map/reduce_scatter | solution.py:683
  138.4 38.6 %collective-permute-start.14 = (bf16[512,1024]{1,0:T(8,128)(2,1)S(1)}, bf16[512,1024]{1,0:T(8,128)(2,1)}, u32[]{:S(2)}, u32[]{:S(2)}) collective-permute-start(bf16[512,1024]{1,0:T(8,128)(2,1)S(1)} %bitcast.61), channel_id=1, source_target_pairs={{0,24},{8,16},{16,8},{24,0},{1,25},{9,17},{17,9},{25,1},{2,26},{10... | collective-permute-start | bytes 3145736 | tf_op jit(solution)/shard_map/ppermute | solution.py:42
  140.1 46.9 %collective-permute-start.13 = (bf16[512,1024]{1,0:T(8,128)(2,1)S(1)}, bf16[512,1024]{1,0:T(8,128)(2,1)}, u32[]{:S(2)}, u32[]{:S(2)}) collective-permute-start(bf16[512,1024]{1,0:T(8,128)(2,1)S(1)} %bitcast.62), channel_id=1, source_target_pairs={{0,16},{8,24},{16,0},{24,8},{1,17},{9,25},{17,1},{25,9},{2,18},{10... | collective-permute-start | bytes 3145736 | tf_op jit(solution)/shard_map/ppermute | solution.py:42
  141.4 45.7 %collective-permute-start.12 = (bf16[512,1024]{1,0:T(8,128)(2,1)S(1)}, bf16[512,1024]{1,0:T(8,128)(2,1)}, u32[]{:S(2)}, u32[]{:S(2)}) collective-permute-start(bf16[512,1024]{1,0:T(8,128)(2,1)S(1)} %bitcast.63), channel_id=1, source_target_pairs={{0,8},{8,0},{16,24},{24,16},{1,9},{9,1},{17,25},{25,17},{2,10},{10... | collective-permute-start | bytes 3145736 | tf_op jit(solution)/shard_map/ppermute | solution.py:42
  208.1 46.4 %collective-permute-start.18 = (bf16[512,1024]{1,0:T(8,128)(2,1)}, bf16[512,1024]{1,0:T(8,128)(2,1)S(1)}, u32[]{:S(2)}, u32[]{:S(2)}) collective-permute-start(bf16[512,1024]{1,0:T(8,128)(2,1)} %get-tuple-element.171), channel_id=1, source_target_pairs={{0,8},{8,0},{16,24},{24,16},{1,9},{9,1},{17,25},{25,17},{2,10},{10... | collective-permute-start | bytes 3145736 | tf_op jit(solution)/shard_map/ppermute | solution.py:42
  209.5 47.5 %collective-permute-start.19 = (bf16[512,1024]{1,0:T(8,128)(2,1)}, bf16[512,1024]{1,0:T(8,128)(2,1)S(1)}, u32[]{:S(2)}, u32[]{:S(2)}) collective-permute-start(bf16[512,1024]{1,0:T(8,128)(2,1)} %get-tuple-element.172), channel_id=1, source_target_pairs={{0,16},{8,24},{16,0},{24,8},{1,17},{9,25},{17,1},{25,9},{2,18},{10... | collective-permute-start | bytes 3145736 | tf_op jit(solution)/shard_map/ppermute | solution.py:42
  210.3 46.7 %collective-permute-start.20 = (bf16[512,1024]{1,0:T(8,128)(2,1)}, bf16[512,1024]{1,0:T(8,128)(2,1)S(1)}, u32[]{:S(2)}, u32[]{:S(2)}) collective-permute-start(bf16[512,1024]{1,0:T(8,128)(2,1)} %get-tuple-element.173), channel_id=1, source_target_pairs={{0,24},{8,16},{16,8},{24,0},{1,25},{9,17},{17,9},{25,1},{2,26},{10... | collective-permute-start | bytes 3145736 | tf_op jit(solution)/shard_map/ppermute | solution.py:42
  218.0 1.8 collective-permute-start.15
  218.0 36.5 %collective-permute-start.16 = (bf16[64,2048]{1,0:T(8,128)(2,1)}, bf16[64,2048]{1,0:T(8,128)(2,1)S(1)}, u32[]{:S(2)}, u32[]{:S(2)}) collective-permute-start(bf16[64,2048]{1,0:T(8,128)(2,1)} %get-tuple-element.168), channel_id=1, source_target_pairs={{0,2},{1,3},{2,0},{3,1},{4,6},{5,7},{6,4},{7,5},{8,10},{9,11},{10,... | collective-permute-start | bytes 786440 | tf_op jit(solution)/shard_map/ppermute | solution.py:46
  219.7 34.8 %collective-permute-start.17 = (bf16[64,2048]{1,0:T(8,128)(2,1)}, bf16[64,2048]{1,0:T(8,128)(2,1)S(1)}, u32[]{:S(2)}, u32[]{:S(2)}) collective-permute-start(bf16[64,2048]{1,0:T(8,128)(2,1)} %get-tuple-element.169), channel_id=1, source_target_pairs={{0,3},{1,2},{2,1},{3,0},{4,7},{5,6},{6,5},{7,4},{8,11},{9,10},{10,... | collective-permute-start | bytes 786440 | tf_op jit(solution)/shard_map/ppermute | solution.py:46
  259.3 31.2 %all-to-all-start.3 = ((bf16[8,64,1024]{2,1,0:T(8,128)(2,1)}), bf16[8,64,1024]{2,1,0:T(8,128)(2,1)S(1)}, u32[]{:S(2)}, u32[]{:S(2)}) async-start(bf16[8,64,1024]{2,1,0:T(8,128)(2,1)} %bitcast.16), calls=%async_computation.3 | async-start | bytes 2097152 | tf_op jit(solution)/shard_map/all_to_all | solution.py:672
  263.9 132.5 %reduce-scatter.5.cloned.1.call-start = ((), (), s32[]{:S(2)}) async-start(), calls=%async_computation.11 | async-start | bytes 4718592 | tf_op jit(solution)/shard_map/reduce_scatter | solution.py:683
  264.0 25.8 %collective-permute-start.21 = (bf16[512,1024]{1,0:T(8,128)(2,1)}, bf16[512,1024]{1,0:T(8,128)(2,1)S(1)}, u32[]{:S(2)}, u32[]{:S(2)}) collective-permute-start(bf16[512,1024]{1,0:T(8,128)(2,1)} %get-tuple-element.175), channel_id=1, source_target_pairs={{0,8},{8,0},{16,24},{24,16},{1,9},{9,1},{17,25},{25,17},{2,10},{10... | collective-permute-start | bytes 3145736 | tf_op jit(solution)/shard_map/ppermute | solution.py:42
  264.7 25.4 %collective-permute-start.22 = (bf16[512,1024]{1,0:T(8,128)(2,1)}, bf16[512,1024]{1,0:T(8,128)(2,1)S(1)}, u32[]{:S(2)}, u32[]{:S(2)}) collective-permute-start(bf16[512,1024]{1,0:T(8,128)(2,1)} %get-tuple-element.177), channel_id=1, source_target_pairs={{0,16},{8,24},{16,0},{24,8},{1,17},{9,25},{17,1},{25,9},{2,18},{10... | collective-permute-start | bytes 3145736 | tf_op jit(solution)/shard_map/ppermute | solution.py:42
  290.6 27.1 %collective-permute-start.26 = (bf16[512,1024]{1,0:T(8,128)(2,1)}, bf16[512,1024]{1,0:T(8,128)(2,1)}, u32[]{:S(2)}, u32[]{:S(2)}) collective-permute-start(bf16[512,1024]{1,0:T(8,128)(2,1)} %get-tuple-element.187), channel_id=1, source_target_pairs={{0,24},{8,16},{16,8},{24,0},{1,25},{9,17},{17,9},{25,1},{2,26},{10... | collective-permute-start | bytes 3145736 | tf_op jit(solution)/shard_map/ppermute | solution.py:42
  308.4 17.7 %collective-permute-start.25 = (f32[12288]{0:T(1024)S(1)}, f32[12288]{0:T(1024)S(1)}, u32[]{:S(2)}, u32[]{:S(2)}) collective-permute-start(f32[12288]{0:T(1024)S(1)} %constant_dynamic-update-slice_fusion), channel_id=1, source_target_pairs={{0,24},{8,16},{16,8},{24,0},{1,25},{9,17},{17,9},{25,1},{2,26},{10... | collective-permute-start | bytes 147464 | tf_op jit(solution)/shard_map/ppermute | solution.py:42
  309.4 16.7 %collective-permute-start.24 = (f32[12288]{0:T(1024)S(1)}, f32[12288]{0:T(1024)S(1)}, u32[]{:S(2)}, u32[]{:S(2)}) collective-permute-start(f32[12288]{0:T(1024)S(1)} %constant_dynamic-update-slice_fusion), channel_id=1, source_target_pairs={{0,16},{8,24},{16,0},{24,8},{1,17},{9,25},{17,1},{25,9},{2,18},{10... | collective-permute-start | bytes 147464 | tf_op jit(solution)/shard_map/ppermute | solution.py:42
  310.8 15.3 %collective-permute-start.23 = (f32[12288]{0:T(1024)S(1)}, f32[12288]{0:T(1024)S(1)}, u32[]{:S(2)}, u32[]{:S(2)}) collective-permute-start(f32[12288]{0:T(1024)S(1)} %constant_dynamic-update-slice_fusion), channel_id=1, source_target_pairs={{0,8},{8,0},{16,24},{24,16},{1,9},{9,1},{17,25},{25,17},{2,10},{10... | collective-permute-start | bytes 147464 | tf_op jit(solution)/shard_map/ppermute | solution.py:42
  321.8 40.1 %all-to-all-start.4 = ((bf16[8,64,1024]{2,1,0:T(8,128)(2,1)}), bf16[8,64,1024]{2,1,0:T(8,128)(2,1)}, u32[]{:S(2)}, u32[]{:S(2)}) async-start(bf16[8,64,1024]{2,1,0:T(8,128)(2,1)} %bitcast.27), calls=%async_computation.6 | async-start | bytes 2097152 | tf_op jit(solution)/shard_map/all_to_all | solution.py:672
  326.1 4.4 %collective-permute-start.27 = (f32[12288]{0:T(1024)S(1)}, f32[12288]{0:T(1024)S(1)}, u32[]{:S(2)}, u32[]{:S(2)}) collective-permute-start(f32[12288]{0:T(1024)S(1)} %add_add_fusion.1), channel_id=1, source_target_pairs={{0,1},{1,0},{2,3},{3,2},{4,5},{5,4},{6,7},{7,6},{8,9},{9,8},{10,11... | collective-permute-start | bytes 147464 | tf_op jit(solution)/shard_map/ppermute | solution.py:42
  327.1 34.8 %collective-permute-start.28 = (bf16[512,768]{1,0:T(8,128)(2,1)}, bf16[512,768]{1,0:T(8,128)(2,1)S(1)}, u32[]{:S(2)}, u32[]{:S(2)}) collective-permute-start(bf16[512,768]{1,0:T(8,128)(2,1)} %get-tuple-element.195), channel_id=1, source_target_pairs={{0,8},{8,0},{16,24},{24,16},{1,9},{9,1},{17,25},{25,17},{2,10},{10... | collective-permute-start | bytes 2359304 | tf_op jit(solution)/shard_map/ppermute | solution.py:42
  328.0 36.2 %collective-permute-start.29 = (bf16[512,768]{1,0:T(8,128)(2,1)}, bf16[512,768]{1,0:T(8,128)(2,1)S(1)}, u32[]{:S(2)}, u32[]{:S(2)}) collective-permute-start(bf16[512,768]{1,0:T(8,128)(2,1)} %get-tuple-element.197), channel_id=1, source_target_pairs={{0,16},{8,24},{16,0},{24,8},{1,17},{9,25},{17,1},{25,9},{2,18},{10... | collective-permute-start | bytes 2359304 | tf_op jit(solution)/shard_map/ppermute | solution.py:42
  329.2 35.0 %collective-permute-start.30 = (bf16[512,768]{1,0:T(8,128)(2,1)}, bf16[512,768]{1,0:T(8,128)(2,1)S(1)}, u32[]{:S(2)}, u32[]{:S(2)}) collective-permute-start(bf16[512,768]{1,0:T(8,128)(2,1)} %get-tuple-element.199), channel_id=1, source_target_pairs={{0,24},{8,16},{16,8},{24,0},{1,25},{9,17},{17,9},{25,1},{2,26},{10... | collective-permute-start | bytes 2359304 | tf_op jit(solution)/shard_map/ppermute | solution.py:42
  367.6 18.8 %collective-permute-start.36 = (f32[2,12288]{1,0:T(2,128)S(1)}, f32[2,12288]{1,0:T(2,128)S(1)}, u32[]{:S(2)}, u32[]{:S(2)}) collective-permute-start(f32[2,12288]{1,0:T(2,128)S(1)} %pad_maximum_fusion.1), channel_id=1, source_target_pairs={{0,6},{1,7},{2,4},{3,5},{4,2},{5,3},{6,0},{7,1},{8,14},{9,15},{10,... | collective-permute-start | bytes 294920 | tf_op jit(solution)/shard_map/ppermute | solution.py:42
  371.4 16.4 %collective-permute-start.35 = (f32[2,12288]{1,0:T(2,128)S(1)}, f32[2,12288]{1,0:T(2,128)S(1)}, u32[]{:S(2)}, u32[]{:S(2)}) collective-permute-start(f32[2,12288]{1,0:T(2,128)S(1)} %pad_maximum_fusion.1), channel_id=1, source_target_pairs={{0,4},{1,5},{2,6},{3,7},{4,0},{5,1},{6,2},{7,3},{8,12},{9,13},{10,... | collective-permute-start | bytes 294920 | tf_op jit(solution)/shard_map/ppermute | solution.py:42
  371.4 16.4 %collective-permute-start.34 = (f32[2,12288]{1,0:T(2,128)S(1)}, f32[2,12288]{1,0:T(2,128)S(1)}, u32[]{:S(2)}, u32[]{:S(2)}) collective-permute-start(f32[2,12288]{1,0:T(2,128)S(1)} %pad_maximum_fusion.1), channel_id=1, source_target_pairs={{0,2},{1,3},{2,0},{3,1},{4,6},{5,7},{6,4},{7,5},{8,10},{9,11},{10,... | collective-permute-start | bytes 294920 | tf_op jit(solution)/shard_map/ppermute | solution.py:42
  372.0 28.0 %all-to-all-start.5 = ((bf16[8,64,768]{2,1,0:T(8,128)(2,1)}), bf16[8,64,768]{2,1,0:T(8,128)(2,1)S(1)}, u32[]{:S(2)}, u32[]{:S(2)}) async-start(bf16[8,64,768]{2,1,0:T(8,128)(2,1)} %bitcast.28), calls=%async_computation.7 | async-start | bytes 1572864 | tf_op jit(solution)/shard_map/all_to_all | solution.py:672
  377.1 13.7 %collective-permute-start.31 = (bf16[64,2048]{1,0:T(8,128)(2,1)}, bf16[64,2048]{1,0:T(8,128)(2,1)S(1)}, u32[]{:S(2)}, u32[]{:S(2)}) collective-permute-start(bf16[64,2048]{1,0:T(8,128)(2,1)} %get-tuple-element.201), channel_id=1, source_target_pairs={{0,8},{8,0},{16,24},{24,16},{1,9},{9,1},{17,25},{25,17},{2,10},{10... | collective-permute-start | bytes 786440 | tf_op jit(solution)/shard_map/ppermute | solution.py:42
  378.3 12.5 %collective-permute-start.32 = (bf16[64,2048]{1,0:T(8,128)(2,1)S(1)}, bf16[64,2048]{1,0:T(8,128)(2,1)S(1)}, u32[]{:S(2)}, u32[]{:S(2)}) collective-permute-start(bf16[64,2048]{1,0:T(8,128)(2,1)S(1)} %copy-done.40), channel_id=1, source_target_pairs={{0,16},{8,24},{16,0},{24,8},{1,17},{9,25},{17,1},{25,9},{2,18},{10... | collective-permute-start | bytes 786440 | tf_op jit(solution)/shard_map/ppermute | solution.py:42
  386.5 9.1 %collective-permute-start.33 = (bf16[64,2048]{1,0:T(8,128)(2,1)S(1)}, bf16[64,2048]{1,0:T(8,128)(2,1)S(1)}, u32[]{:S(2)}, u32[]{:S(2)}) collective-permute-start(bf16[64,2048]{1,0:T(8,128)(2,1)S(1)} %copy-done.39), channel_id=1, source_target_pairs={{0,24},{8,16},{16,8},{24,0},{1,25},{9,17},{17,9},{25,1},{2,26},{10... | collective-permute-start | bytes 786440 | tf_op jit(solution)/shard_map/ppermute | solution.py:42
  (40 other events, 821.8 us)
Sparse Core Ops, SparseCore 0:
  80.5 67.3 all-gather.2
  149.5 45.2 all-gather.4
  197.9 61.5 reduce-scatter.2
  290.7 58.2 reduce-scatter.4
where the time goes:
time: 414 us; the launch traced here: 412 us
  Pallas kernels  165 us (40%)
  waiting for transfers between devices  135 us (33%)
  starting transfers between devices  71.9 us (17%)
  between operations  14.4 us (3%)
  local copies, waits for them, and re-layouts  13.2 us (3%)
  other arithmetic  12.1 us (3%)
    pallas_call x23, Pallas kernels, call(): pl.pallas_call(body, name=getattr(body, 'func', body).__name__, grid_spec...  160 us
    ppermute x31, waiting for transfers between devices, swap(): return lax.ppermute(field, axis, [(i, i ^ bit) for i in range(size)])  84 us
    ppermute x31, starting transfers between devices, swap(): return lax.ppermute(field, axis, [(i, i ^ bit) for i in range(size)])  36.9 us
    all_to_all x6, starting transfers between devices, exchange(): return lax.all_to_all(field, 'blk', 0, 0)  28.6 us
    all_to_all x6, waiting for transfers between devices, exchange(): return lax.all_to_all(field, 'blk', 0, 0)  27.2 us
    ppermute x6, waiting for transfers between devices, swap_group(): return lax.ppermute(field, 'blk', [(i, i ^ bits) for i in range(plan.blks)])  19.1 us
  transfers between devices with their start and end apart: 47, of which 23 were waited for; matrix products, arithmetic and copies ran while one was open for 4% of the time, Pallas kernels for 38%

commit v1 on v0

--- a/solution.py
+++ b/solution.py
@@ -50,12 +50,92 @@
     return [own] + [swap(own, "row", plan.rows, k) for k in range(1, plan.rows)]
 
 
-def scatter_row(pieces, plan, far=None):
-    return [
-        swap(v, "row", plan.rows, k)
-        for k, v in enumerate(pieces)
-        if k and (far is None or far == (k & (k - 1) != 0))
-    ]
+def bits_of(size):
+    return [1 << i for i in range(size.bit_length() - 1)]
+
+
+def near(k):
+    return k & (k - 1) == 0
+
+
+def orders(plan):
+    bits = bits_of(plan.rows)
+    return bits, bits[::-1]
+
+
+def half_of(field, h):
+    middle = field.shape[0] // 2
+    return field[h * middle : (h + 1) * middle]
+
+
+class Gather:
+    def __init__(self, own, plan):
+        self.plan = plan
+        self.whole = {0: own}
+        for bit in bits_of(plan.rows):
+            self.whole[bit] = swap(own, "row", plan.rows, bit)
+
+    def first(self):
+        return [v for k, v in self.whole.items() if k]
+
+    def finish(self, *others):
+        plan = self.plan
+        halves = []
+        for h, order in enumerate(orders(plan)):
+            got = {0: None}
+            for bit in order:
+                for k in list(got):
+                    if k == 0:
+                        got[bit] = half_of(after(self.whole[bit], *others), h)
+                    else:
+                        got[k ^ bit] = swap(got[k], "row", plan.rows, bit)
+            halves.append(got)
+        out = []
+        for k in range(plan.rows):
+            out += [self.whole[k]] if near(k) else [half[k] for half in halves]
+        return out
+
+
+class Scatter:
+    def __init__(self, pieces, plan):
+        self.plan = plan
+        self.whole, far = {}, [{}, {}]
+        for k, piece in enumerate(pieces):
+            if near(k):
+                self.whole[k] = piece
+            else:
+                far[0][k], far[1][k] = half_of(piece, 0), half_of(piece, 1)
+        self.got = []
+        for h, order in enumerate(orders(plan)):
+            held = far[h]
+            for bit in order:
+                for k in [k for k in held if k & bit]:
+                    term = swap(held.pop(k), "row", plan.rows, bit)
+                    if near(k ^ bit):
+                        self.got.append((k ^ bit, h, term))
+                    else:
+                        held[k ^ bit] = (held[k ^ bit].astype(F32) + term.astype(F32)).astype(BF)
+
+    def first(self):
+        return [term for _, _, term in self.got]
+
+    def second(self, turns, *others):
+        got = [(k, h, after(term, *others)) for k, h, term in self.got]
+        while got:
+            first = {}
+            for item in got:
+                first.setdefault(item[0], item)
+            got = [item for item in got if all(item is not v for v in first.values())]
+            sums = add_halves(turns, [(self.whole[k], h, term) for k, h, term in first.values()])
+            self.whole.update(zip(first, sums))
+        return [v for k, v in self.whole.items() if k]
+
+    def finish(self):
+        return [swap(self.whole[bit], "row", self.plan.rows, bit) for bit in bits_of(self.plan.rows)]
+
+
+def scatter_row(pieces, plan):
+    return [swap(pieces[k], "row", plan.rows, k) for k in range(1, plan.rows)]
 
 
 def dot(left, right, left_dim, right_dim):
@@ -91,6 +171,33 @@
 
 def rows_block(columns, block=BLOCK):
     return pl.BlockSpec((block, columns), lambda i, t: (i, 0))
+
+
+def halves_kernel(count, t_ref, *refs):
+    for i in range(count):
+        into, term, out = refs[i], refs[count + i], refs[2 * count + i]
+        out[...] = (into[...].astype(F32) + term[...].astype(F32)).astype(BF)
+
+
+def add_halves(turns, items):
+    count = len(items)
+    depth, width = items[0][2].shape
+    parts = 2
+    into = [pl.BlockSpec((depth, width // parts), lambda i, t, h=h: (h, i)) for _, h, _ in items]
+    term = pl.BlockSpec((depth, width // parts), lambda i, t: (0, i))
+    return pl.pallas_call(
+        functools.partial(halves_kernel, count),
+        name="halves_kernel",
+        grid_spec=pltpu.PrefetchScalarGridSpec(
+            num_scalar_prefetch=1, grid=(parts,), in_specs=into + [term] * count, out_specs=into
+        ),
+        out_shape=[like(v.shape) for v, _, _ in items],
+        input_output_aliases={1 + i: i for i in range(count)},
+        compiler_params=pltpu.CompilerParams(vmem_limit_bytes=SMALL),
+        cost_estimate=pl.CostEstimate(
+            flops=0, bytes_accessed=6 * depth * width * count // COST, transcendentals=0
+        ),
+    )(turns, *[v for v, _, _ in items], *[v for _, _, v in items])
 
 
 def add_kernel(t_ref, *refs):
@@ -434,24 +541,27 @@
     )(jnp.concatenate([turns, places]), attended, grad)
 
 
-def turned_columns(t_ref, w_ref, k, depth):
-    return w_ref[:, pl.ds(pl.multiple_of(t_ref[k] * depth, LANES), depth)]
-
-
-def sum_kernel(t_ref, h_ref, o_ref, w_ref, *refs):
+def turned_columns(t_ref, w_ref, start, size, depth):
+    at = t_ref[start // depth] * depth + start % depth
+    return w_ref[:, pl.ds(pl.multiple_of(at, LANES), size)]
+
+
+def sum_kernel(depth, t_ref, h_ref, o_ref, w_ref, *refs):
     pieces, y_ref = refs[:-1], refs[-1]
-    for k, piece in enumerate(pieces):
-        depth = piece.shape[0]
+    start = 0
+    for piece in pieces:
+        size = piece.shape[0]
         term = dot(h_ref[...], piece[...], 1, 1)
-        term += dot(o_ref[...], turned_columns(t_ref, w_ref, k, depth), 1, 0)
-        y_ref[:, k * depth : (k + 1) * depth] = term.astype(BF)
+        term += dot(o_ref[...], turned_columns(t_ref, w_ref, start, size, depth), 1, 0)
+        y_ref[:, start : start + size] = term.astype(BF)
+        start += size
 
 
 def out_sum(turns, hidden, pieces, attended, out_w):
     count = hidden.shape[0]
     width = out_w.shape[1]
     return call(
-        sum_kernel,
+        functools.partial(sum_kernel, width // turns.shape[0]),
         turns,
         count // BLOCK,
         [rows_block(hidden.shape[1]), rows_block(HD), whole(out_w)] + [whole(p) for p in pieces],
@@ -535,7 +645,7 @@
     heads_grad = None
     for k in range(parts):
         cols = slice(k * depth, (k + 1) * depth)
-        term = dot(g_ref[:, cols], turned_columns(t_ref, w_ref, k, depth), 1, 1)
+        term = dot(g_ref[:, cols], turned_columns(t_ref, w_ref, k * depth, depth, depth), 1, 1)
         heads_grad = term if heads_grad is None else heads_grad + term
     heads_grad = heads_grad.astype(BF)
     allowed = allowed_pairs(g_ref.shape[0], dq_ref, dk_ref)
@@ -738,7 +848,7 @@
     )
     pairs, up_pieces = pairs[: -len(up_pieces)], pairs[-len(up_pieces) :]
     g_all = gather_blocks(g_own)
-    down_pieces = gather_row(down_mine.reshape(-1, own_hidden), plan)
+    down_gather = Gather(down_mine.reshape(-1, own_hidden), plan)
     normed1, normed2 = norms(turns, x_all, vectors)
 
     def own(field):
@@ -756,7 +866,9 @@
     qkv, attended, lse = head_forward(
         turns, own_normed1, qkv_b, pairs, qkv_pieces, length
     )
-    hidden, slope = feed_up(turns, after(normed2, attended), up_b, up_pieces)
+    down_first = down_gather.first()
+    hidden, slope = feed_up(turns, after(normed2, attended, *down_first), up_b, up_pieces)
+    down_pieces = down_gather.finish(attended, *down_first)
     out_term = out_sum(turns, hidden, down_pieces, spread(attended), out_w)
     out_total = sum_blocks(out_term)
 
@@ -773,7 +885,7 @@
     )
     down_total = add_pieces(turns, [after(down_g[0], qkv_grad, *out_got)] + down_got)
     down_back = collect(down_total)
-    up_near = scatter_row([after(v, down_total) for v in up_g], plan, False)
+    up_scatter = Scatter([after(v, down_total) for v in up_g], plan)
     norm_term = norm_back(
         turns,
         after(pre_grad, down_total),
@@ -782,7 +894,8 @@
         qkv_pieces,
         vectors,
     )
-    up_got = up_near + scatter_row([after(v, norm_term, *up_near) for v in up_g], plan, True)
+    up_near = up_scatter.second(turns, norm_term)
+    up_got = up_scatter.finish()
     norm_total = sum_blocks(after(norm_term, down_back, *up_near))
     qkv_g, qkv_parts = weight_grad(
         turns,

time: 414 us -> 408 us (0.986)
  waiting for transfers between devices: 135 us -> 128 us
    ppermute x31 -> x33, waiting for transfers between devices: 84 us -> 66.8 us  [swap(): return lax.ppermute(field, axis, [(i, i ^ bit) for i in range(size)])]
    all_to_all x6, waiting for transfers between devices: 27.2 us -> 34.5 us  [exchange(): return lax.all_to_all(field, 'blk', 0, 0)]
    ppermute x31 -> x33, starting transfers between devices: 36.9 us -> 38.3 us  [swap(): return lax.ppermute(field, axis, [(i, i ^ bit) for i in range(size)])]
    unnamed x93 -> x99, local copies, waits for them, and re-layouts: 8.24 us -> 9.04 us
  transfers between devices with their start and end apart: 47 -> 49, of which waited for: 23 -> 22; matrix products, arithmetic and copies ran while one was open for 4% -> 5% of each run, Pallas kernels for 38% -> 39%
where the time goes in v1:
time: 408 us; the launch traced here: 406 us
  Pallas kernels  166 us (41%)
  waiting for transfers between devices  128 us (31%)
  starting transfers between devices  69.5 us (17%)
  local copies, waits for them, and re-layouts  16.3 us (4%)
  between operations  14.4 us (4%)
  other arithmetic  12.1 us (3%)
    pallas_call x23, Pallas kernels, call(): pl.pallas_call(body, name=getattr(body, 'func', body).__name__, grid_spec...  158 us
    ppermute x33, waiting for transfers between devices, swap(): return lax.ppermute(field, axis, [(i, i ^ bit) for i in range(size)])  66.8 us
    ppermute x33, starting transfers between devices, swap(): return lax.ppermute(field, axis, [(i, i ^ bit) for i in range(size)])  38.3 us
    all_to_all x6, waiting for transfers between devices, exchange(): return lax.all_to_all(field, 'blk', 0, 0)  34.5 us
    all_to_all x6, starting transfers between devices, exchange(): return lax.all_to_all(field, 'blk', 0, 0)  27.5 us
    ppermute x6, waiting for transfers between devices, swap_group(): return lax.ppermute(field, 'blk', [(i, i ^ bits) for i in range(plan.blks)])  20.6 us
    unnamed x99, local copies, waits for them, and re-layouts  9.04 us
  transfers between devices with their start and end apart: 49, of which 22 were waited for; matrix products, arithmetic and copies ran while one was open for 5% of the time, Pallas kernels for 39%

profile of v1, /device:TPU:0, one launch (start us, length us, event | category | flops | bytes accessed | tf_op | source)
XLA Modules:
  0.0 406.2 jit_solution(17015488622181448179)
XLA Ops:
  8.5 3.3 split_attn_kernel.1
  11.7 6.3 %all-to-all-start = ((bf16[8,64,768]{2,1,0:T(8,128)(2,1)}), bf16[8,64,768]{2,1,0:T(8,128)(2,1)S(1)}, u32[]{:S(2)}, u32[]{:S(2)}) async-start(bf16[8,64,768]{2,1,0:T(8,128)(2,1)} %get-tuple-element.116), calls=%async_computation | async-start | bytes 1572864 | tf_op jit(solution)/shard_map/all_to_all | solution.py:782
  18.0 2.4 collective-permute-start.2
  21.5 8.4 %split_kernel.1 = (bf16[8,64,1024]{2,1,0:T(8,128)(2,1)}, bf16[8,64,1024]{2,1,0:T(8,128)(2,1)}) custom-call(s32[4]{0:T(128)} %copy-done.5, bf16[64,2,8192]{2,1,0:T(2,128)(2,1)} %w_ref.2), custom_call_target="tpu_custom_call" | custom-call | bytes 41943 | tf_op jit(solution)/shard_map/split_kernel/pallas_call | solution.py:158
  30.5 2.8 collective-permute-done.1.refs_2_
  34.7 3.0 pick_kernel.2
  39.0 3.6 all-to-all-start.1
  42.6 2.5 collective-permute-start.5
  50.4 4.2 %turn_kernel.1 = (bf16[128,2048]{1,0:T(8,128)(2,1)}, bf16[128,2048]{1,0:T(8,128)(2,1)}, f32[8,2048]{1,0:T(8,128)}, f32[1,2048]{1,0:T(1,128)}) custom-call(s32[4]{0:T(128)} %copy-done.5, bf16[128,2048]{1,0:T(8,128)(2,1)} %bitcast.70, bf16[128,2048]{1,0:T(8,128)(2,1)} %bitcast.71, f32[8,2048]{1,0:T(8,128)} %concatenate.12.v_ref), custom_call_target="tpu_custom_call" | custom-call | bytes 22364 | tf_op jit(solution)/shard_map/turn_kernel/pallas_call | solution.py:158
  54.6 11.9 %collective-permute-done.7.refs_2_ = bf16[64,2048]{1,0:T(8,128)(2,1)} collective-permute-done((bf16[64,2048]{1,0:T(8,128)(2,1)}, bf16[64,2048]{1,0:T(8,128)(2,1)}, u32[]{:S(2)}, u32[]{:S(2)}) %collective-permute-start.7) | collective-permute-done | bytes 262176 | tf_op jit(solution)/shard_map/ppermute | solution.py:46
  66.5 7.0 %collective-permute-done.8.refs_3_ = bf16[64,2048]{1,0:T(8,128)(2,1)} collective-permute-done((bf16[64,2048]{1,0:T(8,128)(2,1)}, bf16[64,2048]{1,0:T(8,128)(2,1)}, u32[]{:S(2)}, u32[]{:S(2)}) %collective-permute-start.8) | collective-permute-done | bytes 262176 | tf_op jit(solution)/shard_map/ppermute | solution.py:46
  73.5 6.8 %collective-permute-done.4.refs_2_.refs_6_.refs_3_ = bf16[512,768]{1,0:T(8,128)(2,1)S(1)} collective-permute-done((bf16[512,768]{1,0:T(8,128)(2,1)S(1)}, bf16[512,768]{1,0:T(8,128)(2,1)S(1)}, u32[]{:S(2)}, u32[]{:S(2)}) %collective-permute-start.4) | collective-permute-done | bytes 786464 | tf_op jit(solution)/shard_map/ppermute | solution.py:42
  81.1 4.8 %all-to-all-start.2 = ((bf16[8,64,1024]{2,1,0:T(8,128)(2,1)}), bf16[8,64,1024]{2,1,0:T(8,128)(2,1)S(1)}, u32[]{:S(2)}, u32[]{:S(2)}) async-start(bf16[8,64,1024]{2,1,0:T(8,128)(2,1)} %get-tuple-element.135), calls=%async_computation.2 | async-start | bytes 2097152 | tf_op jit(solution)/shard_map/all_to_all | solution.py:782
  92.3 3.2 fusion
  95.5 2.9 place_kernel.1.w_ref
  98.5 16.6 %collective-permute-done.11.refs_3_.refs_4_ = bf16[512,1024]{1,0:T(8,128)(2,1)S(1)} collective-permute-done((bf16[512,1024]{1,0:T(8,128)(2,1)S(1)}, bf16[512,1024]{1,0:T(8,128)(2,1)S(1)}, u32[]{:S(2)}, u32[]{:S(2)}) %collective-permute-start.11) | collective-permute-done | bytes 1048608 | tf_op jit(solution)/shard_map/ppermute | solution.py:42
  115.1 22.0 %collective-permute-done.10.refs_2_.refs_3_ = bf16[512,1024]{1,0:T(8,128)(2,1)S(1)} collective-permute-done((bf16[512,1024]{1,0:T(8,128)(2,1)S(1)}, bf16[512,1024]{1,0:T(8,128)(2,1)S(1)}, u32[]{:S(2)}, u32[]{:S(2)}) %collective-permute-start.10) | collective-permute-done | bytes 1048608 | tf_op jit(solution)/shard_map/ppermute | solution.py:42
  142.2 5.8 %all-gather.3.cloned.1.call-done = bf16[2,512,2048]{2,1,0:T(8,128)(2,1)} async-done(((bf16[2,64,2048]{2,1,0:T(8,128)(2,1)}), bf16[2,512,2048]{2,1,0:T(8,128)(2,1)}) %all-gather.3.cloned.1.call-update) | async-done | bytes 4194320 | tf_op jit(solution)/shard_map/all_gather | solution.py:789
  147.9 8.6 %norm_kernel.1 = (bf16[1024,2048]{1,0:T(8,128)(2,1)}, bf16[1024,2048]{1,0:T(8,128)(2,1)}) custom-call(s32[4]{0:T(128)} %copy-done.5, bf16[1024,2048]{1,0:T(8,128)(2,1)} %bitcast.66, f32[8,2048]{1,0:T(8,128)} %get-tuple-element.133.v_ref.o_ref), custom_call_target="tpu_custom_call" | custom-call | flops 419430 | bytes 126484 | tf_op jit(solution)/shard_map/norm_kernel/pallas_call | solution.py:158
  156.5 9.8 %forward_kernel.1 = (bf16[1024,768]{1,0:T(8,128)(2,1)}, bf16[1024,256]{1,0:T(8,128)(2,1)}, f32[1024,1]{1,0:T(8,128)}) custom-call(s32[4]{0:T(128)} %copy-done.5, bf16[1024,2048]{1,0:T(8,128)(2,1)} %get-tuple-element.193.a_ref.l_ref, f32[1,768]{1,0:T(1,128)} %reshape.168.b_ref, f32[2,512,128]{2,1,0:T(8,128)} %get-tuple-element.141.c_ref, ...), custom_call_target="tpu_custom_call" | custom-call | flops 37580964 | bytes 110254 | tf_op jit(solution)/shard_map/forward_kernel/pallas_call | solution.py:158
  170.9 10.9 %up_kernel.1 = (bf16[1024,1024]{1,0:T(8,128)(2,1)}, f32[1024,1024]{1,0:T(8,128)}) custom-call(s32[4]{0:T(128)} %copy-done.5, bf16[1024,2048]{1,0:T(8,128)(2,1)} %get-tuple-element.152.a_ref.l_ref, f32[1,1024]{1,0:T(1,128)} %bitcast.91, bf16[512,1024]{1,0:T(8,128)(2,1)} %bitcast.52, bf16[512,1024]{1,0:T(8,128)(2,1)} %collective-permute-done.9.refs_1_.refs_2_, ...), custom_call_target="tpu_custom_call" | custom-call | flops 42949672 | bytes 146841 | tf_op jit(solution)/shard_map/up_kernel/pallas_call | solution.py:158
  184.6 10.6 %sum_kernel.1 = bf16[1024,2048]{1,0:T(8,128)(2,1)} custom-call(s32[4]{0:T(128)} %copy-done.5, bf16[1024,1024]{1,0:T(8,128)(2,1)} %get-tuple-element.158.h_ref.r_ref, bf16[1024,256]{1,0:T(8,128)(2,1)} %get-tuple-element.150.o_ref, bf16[256,2048]{1,0:T(8,128)(2,1)} %place_kernel.1.w_ref, bf16[512,1024]{1,0:T(8,128)(2,1)} %bitcast.63, ...), custom_call_target="tpu_custom_call" | custom-call | flops 53687092 | bytes 120586 | tf_op jit(solution)/shard_map/sum_kernel/pallas_call | solution.py:158
  195.3 10.2 %weight_kernel.3 = (bf16[512,1024]{1,0:T(8,128)(2,1)}, bf16[512,1024]{1,0:T(8,128)(2,1)}, bf16[512,1024]{1,0:T(8,128)(2,1)}, bf16[512,1024]{1,0:T(8,128)(2,1)}) custom-call(s32[4]{0:T(128)} %copy-done.5, bf16[1024,2048]{1,0:T(8,128)(2,1)} %bitcast.43, bf16[1024,1024]{1,0:T(8,128)(2,1)} %get-tuple-element.158.h_ref.r_ref), custom_call_target="tpu_custom_call" | custom-call | flops 42949672 | bytes 104857 | tf_op jit(solution)/shard_map/weight_kernel/pallas_call | solution.py:158
  209.6 5.8 %out_kernel.1 = (bf16[64,2048]{1,0:T(8,128)(2,1)}, bf16[64,2048]{1,0:T(8,128)(2,1)}, bf16[64,2048]{1,0:T(8,128)(2,1)}, bf16[64,2048]{1,0:T(8,128)(2,1)}) custom-call(s32[8]{0:T(128)} %pad_add_fusion.t_ref, bf16[1024,256]{1,0:T(8,128)(2,1)} %get-tuple-element.150.o_ref, bf16[1024,2048]{1,0:T(8,128)(2,1)} %bitcast.44), custom_call_target="tpu_custom_call" | custom-call | flops 10737418 | bytes 57671 | tf_op jit(solution)/shard_map/out_kernel/pallas_call | solution.py:524
  217.3 10.0 %slope_kernel.1 = (bf16[1024,1024]{1,0:T(8,128)(2,1)}, f32[1,1024]{1,0:T(1,128)}) custom-call(s32[4]{0:T(128)} %copy-done.5, bf16[1024,2048]{1,0:T(8,128)(2,1)} %bitcast.45, f32[1024,1024]{1,0:T(8,128)} %get-tuple-element.167.s_ref, bf16[512,1024]{1,0:T(8,128)(2,1)} %bitcast.64, bf16[512,1024]{1,0:T(8,128)(2,1)} %collective-permute-done.12.refs_1_, ...), custom_call_target="tpu_custom_call" | custom-call | flops 42949672 | bytes 146841 | tf_op jit(solution)/shard_map/slope_kernel/pallas_call | solution.py:158
  227.3 13.4 %weight_kernel.4 = (bf16[512,1024]{1,0:T(8,128)(2,1)}, bf16[512,1024]{1,0:T(8,128)(2,1)}, bf16[512,1024]{1,0:T(8,128)(2,1)}, bf16[512,1024]{1,0:T(8,128)(2,1)}, f32[2,2048,128]{2,1,0:T(8,128)}) custom-call(s32[4]{0:T(128)} %copy-done.5, bf16[1024,2048]{1,0:T(8,128)(2,1)} %get-tuple-element.152.a_ref.l_ref, ...), custom_call_target="tpu_custom_call" | custom-call | flops 42949672 | bytes 167813 | tf_op jit(solution)/shard_map/weight_kernel/pallas_call | solution.py:158
  240.6 10.2 %backward_kernel.1 = (bf16[1024,768]{1,0:T(8,128)(2,1)}, f32[1,768]{1,0:T(1,128)}) custom-call(s32[4]{0:T(128)} %copy-done.5, bf16[1024,2048]{1,0:T(8,128)(2,1)} %bitcast.46, bf16[256,2048]{1,0:T(8,128)(2,1)} %place_kernel.1.w_ref, bf16[1024,768]{1,0:T(8,128)(2,1)} %get-tuple-element.172.qkv_ref, bf16[1024,256]{1,0:T(8,128)(2,1)} %get-tuple-element.150.o_ref, ...), custom_call_target="tpu_custom_call" | custom-call | flops 24159192 | bytes 105011 | tf_op jit(solution)/shard_map/backward_kernel/pallas_call | solution.py:158
  250.9 3.3 collective-permute-done.20.refs_2_
  254.1 2.4 add_kernel.3
  256.5 3.6 all-to-all-start.3
  262.4 13.8 %back_kernel.1 = bf16[1024,2048]{1,0:T(8,128)(2,1)} custom-call(s32[4]{0:T(128)} %copy-done.5, bf16[1024,1024]{1,0:T(8,128)(2,1)} %get-tuple-element.188.r_ref.p_ref, bf16[1024,768]{1,0:T(8,128)(2,1)} %get-tuple-element.174.q_ref.r_ref, f32[8,2048]{1,0:T(8,128)} %get-tuple-element.133.v_ref.o_ref, bf16[512,1024]{1,0:T(8,128)(2,1)} %bitcast.54, ...), custom_call_target="tpu_custom_call" | custom-call | flops 75161928 | bytes 152698 | tf_op jit(solution)/shard_map/back_kernel/pallas_call | solution.py:158
  276.2 2.7 halves_kernel.1
  278.9 7.7 %all-to-all-done.3.d_ref = bf16[8,64,1024]{2,1,0:T(8,128)(2,1)S(1)} async-done(((bf16[8,64,1024]{2,1,0:T(8,128)(2,1)}), bf16[8,64,1024]{2,1,0:T(8,128)(2,1)S(1)}, u32[]{:S(2)}, u32[]{:S(2)}) %all-to-all-start.3) | async-done | bytes 1048608 | tf_op jit(solution)/shard_map/all_to_all | solution.py:782
  291.1 11.1 %weight_kernel.5 = (bf16[512,768]{1,0:T(8,128)(2,1)}, bf16[512,768]{1,0:T(8,128)(2,1)}, bf16[512,768]{1,0:T(8,128)(2,1)}, bf16[512,768]{1,0:T(8,128)(2,1)}, f32[2,2048,128]{2,1,0:T(8,128)}) custom-call(s32[4]{0:T(128)} %copy-done.5, bf16[1024,2048]{1,0:T(8,128)(2,1)} %get-tuple-element.193.a_ref.l_ref, bf16[1024,768]{1,0:T(8,128)(2,1)} %get-tuple-element.174.q_ref.r_ref, ...), custom_call_target="tpu_custom_call" | custom-call | flops 32212254 | bytes 141588 | tf_op jit(solution)/shard_map/weight_kernel/pallas_call | solution.py:158
  302.2 2.2 reduce_sum.53
  308.1 4.6 %collective-permute-done.27.refs_1_ = bf16[512,1024]{1,0:T(8,128)(2,1)S(1)} collective-permute-done((bf16[512,1024]{1,0:T(8,128)(2,1)}, bf16[512,1024]{1,0:T(8,128)(2,1)S(1)}, u32[]{:S(2)}, u32[]{:S(2)}) %collective-permute-start.27) | collective-permute-done | bytes 1048608 | tf_op jit(solution)/shard_map/ppermute | solution.py:42
  313.6 2.3 add_kernel.4
  315.9 4.3 %all-to-all-start.4 = ((bf16[8,64,1024]{2,1,0:T(8,128)(2,1)}), bf16[8,64,1024]{2,1,0:T(8,128)(2,1)}, u32[]{:S(2)}, u32[]{:S(2)}) async-start(bf16[8,64,1024]{2,1,0:T(8,128)(2,1)} %bitcast.27), calls=%async_computation.6 | async-start | bytes 2097152 | tf_op jit(solution)/shard_map/all_to_all | solution.py:782
  324.7 2.9 finish_kernel.2
  327.6 3.0 pick_kernel.3
  330.6 25.4 %all-to-all-done.4.u_ref = bf16[8,64,1024]{2,1,0:T(8,128)(2,1)} async-done(((bf16[8,64,1024]{2,1,0:T(8,128)(2,1)}), bf16[8,64,1024]{2,1,0:T(8,128)(2,1)}, u32[]{:S(2)}, u32[]{:S(2)}) %all-to-all-start.4) | async-done | bytes 1048608 | tf_op jit(solution)/shard_map/all_to_all | solution.py:782
  355.9 2.9 collective-permute-done.31.refs_2_
  362.3 3.7 collective-permute-start.38
  366.6 5.0 %all-to-all-start.5 = ((bf16[8,64,768]{2,1,0:T(8,128)(2,1)}), bf16[8,64,768]{2,1,0:T(8,128)(2,1)S(1)}, u32[]{:S(2)}, u32[]{:S(2)}) async-start(bf16[8,64,768]{2,1,0:T(8,128)(2,1)} %bitcast.28), calls=%async_computation.7 | async-start | bytes 1572864 | tf_op jit(solution)/shard_map/all_to_all | solution.py:782
  373.7 7.1 %join_kernel.1 = f32[64,2,8192]{2,1,0:T(2,128)} custom-call(s32[4]{0:T(128)} %copy-done.5, bf16[8,64,1024]{2,1,0:T(8,128)(2,1)} %all-to-all-done.4.u_ref, bf16[8,64,1024]{2,1,0:T(8,128)(2,1)} %copy-done.18), custom_call_target="tpu_custom_call" | custom-call | bytes 62914 | tf_op jit(solution)/shard_map/join_kernel/pallas_call | solution.py:158
  385.3 4.6 %collective-permute-done.35 = bf16[64,2048]{1,0:T(8,128)(2,1)S(1)} collective-permute-done((bf16[64,2048]{1,0:T(8,128)(2,1)S(1)}, bf16[64,2048]{1,0:T(8,128)(2,1)S(1)}, u32[]{:S(2)}, u32[]{:S(2)}) %collective-permute-start.35) | collective-permute-done | bytes 262176 | tf_op jit(solution)/shard_map/ppermute | solution.py:42
  390.8 3.5 finish_kernel.3
  395.3 3.8 join_attn_kernel.1
  (221 shorter events, 65.1 us)
Async XLA Ops:
  11.7 27.3 %all-to-all-start = ((bf16[8,64,768]{2,1,0:T(8,128)(2,1)}), bf16[8,64,768]{2,1,0:T(8,128)(2,1)S(1)}, u32[]{:S(2)}, u32[]{:S(2)}) async-start(bf16[8,64,768]{2,1,0:T(8,128)(2,1)} %get-tuple-element.116), calls=%async_computation | async-start | bytes 1572864 | tf_op jit(solution)/shard_map/all_to_all | solution.py:782
  18.0 12.4 %collective-permute-start.2 = (bf16[64,2048]{1,0:T(8,128)(2,1)S(1)}, bf16[64,2048]{1,0:T(8,128)(2,1)S(1)}, u32[]{:S(2)}, u32[]{:S(2)}) collective-permute-start(bf16[64,2048]{1,0:T(8,128)(2,1)S(1)} %get-tuple-element.119.refs_0_), channel_id=1, source_target_pairs={{0,24},{8,16},{16,8},{24,0},{1,25},{9,17},{17,9},{25,1},{2,26},{10... | collective-permute-start | bytes 786440 | tf_op jit(solution)/shard_map/ppermute | solution.py:42
  20.5 12.8 %collective-permute-start.1 = (bf16[64,2048]{1,0:T(8,128)(2,1)S(1)}, bf16[64,2048]{1,0:T(8,128)(2,1)S(1)}, u32[]{:S(2)}, u32[]{:S(2)}) collective-permute-start(bf16[64,2048]{1,0:T(8,128)(2,1)S(1)} %get-tuple-element.119.refs_0_), channel_id=1, source_target_pairs={{0,16},{8,24},{16,0},{24,8},{1,17},{9,25},{17,1},{25,9},{2,18},{10... | collective-permute-start | bytes 786440 | tf_op jit(solution)/shard_map/ppermute | solution.py:42
  21.0 12.4 %collective-permute-start = (bf16[64,2048]{1,0:T(8,128)(2,1)S(1)}, bf16[64,2048]{1,0:T(8,128)(2,1)S(1)}, u32[]{:S(2)}, u32[]{:S(2)}) collective-permute-start(bf16[64,2048]{1,0:T(8,128)(2,1)S(1)} %get-tuple-element.119.refs_0_), channel_id=1, source_target_pairs={{0,8},{8,0},{16,24},{24,16},{1,9},{9,1},{17,25},{25,17},{2,10},{10... | collective-permute-start | bytes 786440 | tf_op jit(solution)/shard_map/ppermute | solution.py:42
  39.0 41.4 %all-to-all-start.1 = ((bf16[8,64,1024]{2,1,0:T(8,128)(2,1)}), bf16[8,64,1024]{2,1,0:T(8,128)(2,1)S(1)}, u32[]{:S(2)}, u32[]{:S(2)}) async-start(bf16[8,64,1024]{2,1,0:T(8,128)(2,1)} %get-tuple-element.124), calls=%async_computation.1 | async-start | bytes 2097152 | tf_op jit(solution)/shard_map/all_to_all | solution.py:782
  42.6 105.3 %all-gather.3.cloned.1.call-start = ((), (), s32[]{:S(2)}) async-start(), calls=%async_computation.8 | async-start | bytes 4718592 | tf_op jit(solution)/shard_map/all_gather | solution.py:789
  42.6 30.8 %collective-permute-start.5 = (bf16[512,768]{1,0:T(8,128)(2,1)S(1)}, bf16[512,768]{1,0:T(8,128)(2,1)S(1)}, u32[]{:S(2)}, u32[]{:S(2)}) collective-permute-start(bf16[512,768]{1,0:T(8,128)(2,1)S(1)} %bitcast.55), channel_id=1, source_target_pairs={{0,24},{8,16},{16,8},{24,0},{1,25},{9,17},{17,9},{25,1},{2,26},{10... | collective-permute-start | bytes 2359304 | tf_op jit(solution)/shard_map/ppermute | solution.py:42
  45.2 35.0 %collective-permute-start.4 = (bf16[512,768]{1,0:T(8,128)(2,1)S(1)}, bf16[512,768]{1,0:T(8,128)(2,1)S(1)}, u32[]{:S(2)}, u32[]{:S(2)}) collective-permute-start(bf16[512,768]{1,0:T(8,128)(2,1)S(1)} %bitcast.56), channel_id=1, source_target_pairs={{0,16},{8,24},{16,0},{24,8},{1,17},{9,25},{17,1},{25,9},{2,18},{10... | collective-permute-start | bytes 2359304 | tf_op jit(solution)/shard_map/ppermute | solution.py:42
  45.7 34.7 %collective-permute-start.3 = (bf16[512,768]{1,0:T(8,128)(2,1)S(1)}, bf16[512,768]{1,0:T(8,128)(2,1)}, u32[]{:S(2)}, u32[]{:S(2)}) collective-permute-start(bf16[512,768]{1,0:T(8,128)(2,1)S(1)} %bitcast.57), channel_id=1, source_target_pairs={{0,8},{8,0},{16,24},{24,16},{1,9},{9,1},{17,25},{25,17},{2,10},{10... | collective-permute-start | bytes 2359304 | tf_op jit(solution)/shard_map/ppermute | solution.py:42
  46.2 1.9 collective-permute-start.6
  46.2 20.3 %collective-permute-start.7 = (bf16[64,2048]{1,0:T(8,128)(2,1)}, bf16[64,2048]{1,0:T(8,128)(2,1)}, u32[]{:S(2)}, u32[]{:S(2)}) collective-permute-start(bf16[64,2048]{1,0:T(8,128)(2,1)} %get-tuple-element.130), channel_id=1, source_target_pairs={{0,2},{1,3},{2,0},{3,1},{4,6},{5,7},{6,4},{7,5},{8,10},{9,11},{10,... | collective-permute-start | bytes 786440 | tf_op jit(solution)/shard_map/ppermute | solution.py:46
  48.1 25.4 %collective-permute-start.8 = (bf16[64,2048]{1,0:T(8,128)(2,1)}, bf16[64,2048]{1,0:T(8,128)(2,1)}, u32[]{:S(2)}, u32[]{:S(2)}) collective-permute-start(bf16[64,2048]{1,0:T(8,128)(2,1)} %get-tuple-element.131), channel_id=1, source_target_pairs={{0,3},{1,2},{2,1},{3,0},{4,7},{5,6},{6,5},{7,4},{8,11},{9,10},{10,... | collective-permute-start | bytes 786440 | tf_op jit(solution)/shard_map/ppermute | solution.py:46
  81.1 57.1 %all-to-all-start.2 = ((bf16[8,64,1024]{2,1,0:T(8,128)(2,1)}), bf16[8,64,1024]{2,1,0:T(8,128)(2,1)S(1)}, u32[]{:S(2)}, u32[]{:S(2)}) async-start(bf16[8,64,1024]{2,1,0:T(8,128)(2,1)} %get-tuple-element.135), calls=%async_computation.2 | async-start | bytes 2097152 | tf_op jit(solution)/shard_map/all_to_all | solution.py:782
  85.9 109.4 %all-gather.5.cloned.1.call-start = ((), (), s32[]{:S(2)}) async-start(), calls=%async_computation.9 | async-start | bytes 4718592 | tf_op jit(solution)/shard_map/all_gather | solution.py:789
  88.2 26.9 %collective-permute-start.11 = (bf16[512,1024]{1,0:T(8,128)(2,1)S(1)}, bf16[512,1024]{1,0:T(8,128)(2,1)S(1)}, u32[]{:S(2)}, u32[]{:S(2)}) collective-permute-start(bf16[512,1024]{1,0:T(8,128)(2,1)S(1)} %bitcast.49), channel_id=1, source_target_pairs={{0,24},{8,16},{16,8},{24,0},{1,25},{9,17},{17,9},{25,1},{2,26},{10... | collective-permute-start | bytes 3145736 | tf_op jit(solution)/shard_map/ppermute | solution.py:42
  89.9 47.1 %collective-permute-start.10 = (bf16[512,1024]{1,0:T(8,128)(2,1)S(1)}, bf16[512,1024]{1,0:T(8,128)(2,1)S(1)}, u32[]{:S(2)}, u32[]{:S(2)}) collective-permute-start(bf16[512,1024]{1,0:T(8,128)(2,1)S(1)} %bitcast.50), channel_id=1, source_target_pairs={{0,16},{8,24},{16,0},{24,8},{1,17},{9,25},{17,1},{25,9},{2,18},{10... | collective-permute-start | bytes 3145736 | tf_op jit(solution)/shard_map/ppermute | solution.py:42
  91.1 46.9 %collective-permute-start.9 = (bf16[512,1024]{1,0:T(8,128)(2,1)S(1)}, bf16[512,1024]{1,0:T(8,128)(2,1)}, u32[]{:S(2)}, u32[]{:S(2)}) collective-permute-start(bf16[512,1024]{1,0:T(8,128)(2,1)S(1)} %bitcast.51), channel_id=1, source_target_pairs={{0,8},{8,0},{16,24},{24,16},{1,9},{9,1},{17,25},{25,17},{2,10},{10... | collective-permute-start | bytes 3145736 | tf_op jit(solution)/shard_map/ppermute | solution.py:42
  138.2 152.8 %reduce-scatter.3.cloned.1.call-start = ((), (), s32[]{:S(2)}) async-start(), calls=%async_computation.10 | async-start | bytes 4718592 | tf_op jit(solution)/shard_map/reduce_scatter | solution.py:793
  138.2 28.1 %collective-permute-start.13 = (bf16[512,1024]{1,0:T(8,128)(2,1)S(1)}, bf16[512,1024]{1,0:T(8,128)(2,1)}, u32[]{:S(2)}, u32[]{:S(2)}) collective-permute-start(bf16[512,1024]{1,0:T(8,128)(2,1)S(1)} %bitcast.61), channel_id=1, source_target_pairs={{0,16},{8,24},{16,0},{24,8},{1,17},{9,25},{17,1},{25,9},{2,18},{10... | collective-permute-start | bytes 3145736 | tf_op jit(solution)/shard_map/ppermute | solution.py:42
  139.9 26.5 %collective-permute-start.12 = (bf16[512,1024]{1,0:T(8,128)(2,1)S(1)}, bf16[512,1024]{1,0:T(8,128)(2,1)}, u32[]{:S(2)}, u32[]{:S(2)}) collective-permute-start(bf16[512,1024]{1,0:T(8,128)(2,1)S(1)} %bitcast.62), channel_id=1, source_target_pairs={{0,8},{8,0},{16,24},{24,16},{1,9},{9,1},{17,25},{25,17},{2,10},{10... | collective-permute-start | bytes 3145736 | tf_op jit(solution)/shard_map/ppermute | solution.py:42
  168.5 14.1 %collective-permute-start.15 = (bf16[256,1024]{1,0:T(8,128)(2,1)S(1)}, bf16[256,1024]{1,0:T(8,128)(2,1)S(1)}, u32[]{:S(2)}, u32[]{:S(2)}) collective-permute-start(bf16[256,1024]{1,0:T(8,128)(2,1)S(1)} %slice.25), channel_id=1, source_target_pairs={{0,8},{8,0},{16,24},{24,16},{1,9},{9,1},{17,25},{25,17},{2,10},{10... | collective-permute-start | bytes 1572872 | tf_op jit(solution)/shard_map/ppermute | solution.py:42
  170.1 13.8 %collective-permute-start.14 = (bf16[256,1024]{1,0:T(8,128)(2,1)S(1)}, bf16[256,1024]{1,0:T(8,128)(2,1)S(1)}, u32[]{:S(2)}, u32[]{:S(2)}) collective-permute-start(bf16[256,1024]{1,0:T(8,128)(2,1)S(1)} %slice.24), channel_id=1, source_target_pairs={{0,16},{8,24},{16,0},{24,8},{1,17},{9,25},{17,1},{25,9},{2,18},{10... | collective-permute-start | bytes 1572872 | tf_op jit(solution)/shard_map/ppermute | solution.py:42
  205.5 45.3 %collective-permute-start.19 = (bf16[512,1024]{1,0:T(8,128)(2,1)}, bf16[512,1024]{1,0:T(8,128)(2,1)S(1)}, u32[]{:S(2)}, u32[]{:S(2)}) collective-permute-start(bf16[512,1024]{1,0:T(8,128)(2,1)} %get-tuple-element.179), channel_id=1, source_target_pairs={{0,8},{8,0},{16,24},{24,16},{1,9},{9,1},{17,25},{25,17},{2,10},{10... | collective-permute-start | bytes 3145736 | tf_op jit(solution)/shard_map/ppermute | solution.py:42
  206.4 47.7 %collective-permute-start.20 = (bf16[512,1024]{1,0:T(8,128)(2,1)}, bf16[512,1024]{1,0:T(8,128)(2,1)S(1)}, u32[]{:S(2)}, u32[]{:S(2)}) collective-permute-start(bf16[512,1024]{1,0:T(8,128)(2,1)} %get-tuple-element.180), channel_id=1, source_target_pairs={{0,16},{8,24},{16,0},{24,8},{1,17},{9,25},{17,1},{25,9},{2,18},{10... | collective-permute-start | bytes 3145736 | tf_op jit(solution)/shard_map/ppermute | solution.py:42
  207.9 46.2 %collective-permute-start.21 = (bf16[512,1024]{1,0:T(8,128)(2,1)}, bf16[512,1024]{1,0:T(8,128)(2,1)S(1)}, u32[]{:S(2)}, u32[]{:S(2)}) collective-permute-start(bf16[512,1024]{1,0:T(8,128)(2,1)} %get-tuple-element.181), channel_id=1, source_target_pairs={{0,24},{8,16},{16,8},{24,0},{1,25},{9,17},{17,9},{25,1},{2,26},{10... | collective-permute-start | bytes 3145736 | tf_op jit(solution)/shard_map/ppermute | solution.py:42
  215.4 35.4 %collective-permute-start.17 = (bf16[64,2048]{1,0:T(8,128)(2,1)}, bf16[64,2048]{1,0:T(8,128)(2,1)S(1)}, u32[]{:S(2)}, u32[]{:S(2)}) collective-permute-start(bf16[64,2048]{1,0:T(8,128)(2,1)} %get-tuple-element.176), channel_id=1, source_target_pairs={{0,2},{1,3},{2,0},{3,1},{4,6},{5,7},{6,4},{7,5},{8,10},{9,11},{10,... | collective-permute-start | bytes 786440 | tf_op jit(solution)/shard_map/ppermute | solution.py:46
  217.1 33.7 %collective-permute-start.18 = (bf16[64,2048]{1,0:T(8,128)(2,1)}, bf16[64,2048]{1,0:T(8,128)(2,1)S(1)}, u32[]{:S(2)}, u32[]{:S(2)}) collective-permute-start(bf16[64,2048]{1,0:T(8,128)(2,1)} %get-tuple-element.177), channel_id=1, source_target_pairs={{0,3},{1,2},{2,1},{3,0},{4,7},{5,6},{6,5},{7,4},{8,11},{9,10},{10,... | collective-permute-start | bytes 786440 | tf_op jit(solution)/shard_map/ppermute | solution.py:46
  256.5 30.1 %all-to-all-start.3 = ((bf16[8,64,1024]{2,1,0:T(8,128)(2,1)}), bf16[8,64,1024]{2,1,0:T(8,128)(2,1)S(1)}, u32[]{:S(2)}, u32[]{:S(2)}) async-start(bf16[8,64,1024]{2,1,0:T(8,128)(2,1)} %bitcast.16), calls=%async_computation.3 | async-start | bytes 2097152 | tf_op jit(solution)/shard_map/all_to_all | solution.py:782
  260.1 130.7 %reduce-scatter.5.cloned.1.call-start = ((), (), s32[]{:S(2)}) async-start(), calls=%async_computation.11 | async-start | bytes 4718592 | tf_op jit(solution)/shard_map/reduce_scatter | solution.py:793
  260.3 15.9 %collective-permute-start.23 = (bf16[256,1024]{1,0:T(8,128)(2,1)S(1)}, bf16[256,1024]{1,0:T(8,128)(2,1)S(1)}, u32[]{:S(2)}, u32[]{:S(2)}) collective-permute-start(bf16[256,1024]{1,0:T(8,128)(2,1)S(1)} %get-tuple-element.224), channel_id=1, source_target_pairs={{0,16},{8,24},{16,0},{24,8},{1,17},{9,25},{17,1},{25,9},{2,18},{10... | collective-permute-start | bytes 1572872 | tf_op jit(solution)/shard_map/ppermute | solution.py:42
  261.8 14.4 %collective-permute-start.22 = (bf16[256,1024]{1,0:T(8,128)(2,1)S(1)}, bf16[256,1024]{1,0:T(8,128)(2,1)S(1)}, u32[]{:S(2)}, u32[]{:S(2)}) collective-permute-start(bf16[256,1024]{1,0:T(8,128)(2,1)S(1)} %get-tuple-element.225), channel_id=1, source_target_pairs={{0,8},{8,0},{16,24},{24,16},{1,9},{9,1},{17,25},{25,17},{2,10},{10... | collective-permute-start | bytes 1572872 | tf_op jit(solution)/shard_map/ppermute | solution.py:42
  286.7 26.0 %collective-permute-start.27 = (bf16[512,1024]{1,0:T(8,128)(2,1)}, bf16[512,1024]{1,0:T(8,128)(2,1)S(1)}, u32[]{:S(2)}, u32[]{:S(2)}) collective-permute-start(bf16[512,1024]{1,0:T(8,128)(2,1)} %get-tuple-element.191), channel_id=1, source_target_pairs={{0,8},{8,0},{16,24},{24,16},{1,9},{9,1},{17,25},{25,17},{2,10},{10... | collective-permute-start | bytes 3145736 | tf_op jit(solution)/shard_map/ppermute | solution.py:42
  287.9 25.7 %collective-permute-start.28 = (bf16[512,1024]{1,0:T(8,128)(2,1)}, bf16[512,1024]{1,0:T(8,128)(2,1)S(1)}, u32[]{:S(2)}, u32[]{:S(2)}) collective-permute-start(bf16[512,1024]{1,0:T(8,128)(2,1)} %get-tuple-element.192), channel_id=1, source_target_pairs={{0,16},{8,24},{16,0},{24,8},{1,17},{9,25},{17,1},{25,9},{2,18},{10... | collective-permute-start | bytes 3145736 | tf_op jit(solution)/shard_map/ppermute | solution.py:42
  304.5 15.6 %collective-permute-start.26 = (f32[12288]{0:T(1024)S(1)}, f32[12288]{0:T(1024)S(1)}, u32[]{:S(2)}, u32[]{:S(2)}) collective-permute-start(f32[12288]{0:T(1024)S(1)} %constant_dynamic-update-slice_fusion), channel_id=1, source_target_pairs={{0,24},{8,16},{16,8},{24,0},{1,25},{9,17},{17,9},{25,1},{2,26},{10... | collective-permute-start | bytes 147464 | tf_op jit(solution)/shard_map/ppermute | solution.py:42
  306.1 14.1 %collective-permute-start.25 = (f32[12288]{0:T(1024)S(1)}, f32[12288]{0:T(1024)S(1)}, u32[]{:S(2)}, u32[]{:S(2)}) collective-permute-start(f32[12288]{0:T(1024)S(1)} %constant_dynamic-update-slice_fusion), channel_id=1, source_target_pairs={{0,16},{8,24},{16,0},{24,8},{1,17},{9,25},{17,1},{25,9},{2,18},{10... | collective-permute-start | bytes 147464 | tf_op jit(solution)/shard_map/ppermute | solution.py:42
  307.5 12.6 %collective-permute-start.24 = (f32[12288]{0:T(1024)S(1)}, f32[12288]{0:T(1024)S(1)}, u32[]{:S(2)}, u32[]{:S(2)}) collective-permute-start(f32[12288]{0:T(1024)S(1)} %constant_dynamic-update-slice_fusion), channel_id=1, source_target_pairs={{0,8},{8,0},{16,24},{24,16},{1,9},{9,1},{17,25},{25,17},{2,10},{10... | collective-permute-start | bytes 147464 | tf_op jit(solution)/shard_map/ppermute | solution.py:42
  315.9 40.1 %all-to-all-start.4 = ((bf16[8,64,1024]{2,1,0:T(8,128)(2,1)}), bf16[8,64,1024]{2,1,0:T(8,128)(2,1)}, u32[]{:S(2)}, u32[]{:S(2)}) async-start(bf16[8,64,1024]{2,1,0:T(8,128)(2,1)} %bitcast.27), calls=%async_computation.6 | async-start | bytes 2097152 | tf_op jit(solution)/shard_map/all_to_all | solution.py:782
  320.2 4.4 %collective-permute-start.29 = (f32[12288]{0:T(1024)S(1)}, f32[12288]{0:T(1024)S(1)}, u32[]{:S(2)}, u32[]{:S(2)}) collective-permute-start(f32[12288]{0:T(1024)S(1)} %add_add_fusion.1), channel_id=1, source_target_pairs={{0,1},{1,0},{2,3},{3,2},{4,5},{5,4},{6,7},{7,6},{8,9},{9,8},{10,11... | collective-permute-start | bytes 147464 | tf_op jit(solution)/shard_map/ppermute | solution.py:42
  321.1 34.8 %collective-permute-start.30 = (bf16[512,768]{1,0:T(8,128)(2,1)}, bf16[512,768]{1,0:T(8,128)(2,1)S(1)}, u32[]{:S(2)}, u32[]{:S(2)}) collective-permute-start(bf16[512,768]{1,0:T(8,128)(2,1)} %get-tuple-element.207), channel_id=1, source_target_pairs={{0,8},{8,0},{16,24},{24,16},{1,9},{9,1},{17,25},{25,17},{2,10},{10... | collective-permute-start | bytes 2359304 | tf_op jit(solution)/shard_map/ppermute | solution.py:42
  322.5 36.4 %collective-permute-start.31 = (bf16[512,768]{1,0:T(8,128)(2,1)}, bf16[512,768]{1,0:T(8,128)(2,1)S(1)}, u32[]{:S(2)}, u32[]{:S(2)}) collective-permute-start(bf16[512,768]{1,0:T(8,128)(2,1)} %get-tuple-element.209), channel_id=1, source_target_pairs={{0,16},{8,24},{16,0},{24,8},{1,17},{9,25},{17,1},{25,9},{2,18},{10... | collective-permute-start | bytes 2359304 | tf_op jit(solution)/shard_map/ppermute | solution.py:42
  324.0 34.9 %collective-permute-start.32 = (bf16[512,768]{1,0:T(8,128)(2,1)}, bf16[512,768]{1,0:T(8,128)(2,1)S(1)}, u32[]{:S(2)}, u32[]{:S(2)}) collective-permute-start(bf16[512,768]{1,0:T(8,128)(2,1)} %get-tuple-element.211), channel_id=1, source_target_pairs={{0,24},{8,16},{16,8},{24,0},{1,25},{9,17},{17,9},{25,1},{2,26},{10... | collective-permute-start | bytes 2359304 | tf_op jit(solution)/shard_map/ppermute | solution.py:42
  362.3 18.6 %collective-permute-start.38 = (f32[2,12288]{1,0:T(2,128)S(1)}, f32[2,12288]{1,0:T(2,128)S(1)}, u32[]{:S(2)}, u32[]{:S(2)}) collective-permute-start(f32[2,12288]{1,0:T(2,128)S(1)} %pad_maximum_fusion.1), channel_id=1, source_target_pairs={{0,6},{1,7},{2,4},{3,5},{4,2},{5,3},{6,0},{7,1},{8,14},{9,15},{10,... | collective-permute-start | bytes 294920 | tf_op jit(solution)/shard_map/ppermute | solution.py:42
  366.0 16.4 %collective-permute-start.37 = (f32[2,12288]{1,0:T(2,128)S(1)}, f32[2,12288]{1,0:T(2,128)S(1)}, u32[]{:S(2)}, u32[]{:S(2)}) collective-permute-start(f32[2,12288]{1,0:T(2,128)S(1)} %pad_maximum_fusion.1), channel_id=1, source_target_pairs={{0,4},{1,5},{2,6},{3,7},{4,0},{5,1},{6,2},{7,3},{8,12},{9,13},{10,... | collective-permute-start | bytes 294920 | tf_op jit(solution)/shard_map/ppermute | solution.py:42
  366.0 16.4 %collective-permute-start.36 = (f32[2,12288]{1,0:T(2,128)S(1)}, f32[2,12288]{1,0:T(2,128)S(1)}, u32[]{:S(2)}, u32[]{:S(2)}) collective-permute-start(f32[2,12288]{1,0:T(2,128)S(1)} %pad_maximum_fusion.1), channel_id=1, source_target_pairs={{0,2},{1,3},{2,0},{3,1},{4,6},{5,7},{6,4},{7,5},{8,10},{9,11},{10,... | collective-permute-start | bytes 294920 | tf_op jit(solution)/shard_map/ppermute | solution.py:42
  366.6 27.7 %all-to-all-start.5 = ((bf16[8,64,768]{2,1,0:T(8,128)(2,1)}), bf16[8,64,768]{2,1,0:T(8,128)(2,1)S(1)}, u32[]{:S(2)}, u32[]{:S(2)}) async-start(bf16[8,64,768]{2,1,0:T(8,128)(2,1)} %bitcast.28), calls=%async_computation.7 | async-start | bytes 1572864 | tf_op jit(solution)/shard_map/all_to_all | solution.py:782
  371.6 13.7 %collective-permute-start.33 = (bf16[64,2048]{1,0:T(8,128)(2,1)}, bf16[64,2048]{1,0:T(8,128)(2,1)S(1)}, u32[]{:S(2)}, u32[]{:S(2)}) collective-permute-start(bf16[64,2048]{1,0:T(8,128)(2,1)} %get-tuple-element.213), channel_id=1, source_target_pairs={{0,8},{8,0},{16,24},{24,16},{1,9},{9,1},{17,25},{25,17},{2,10},{10... | collective-permute-start | bytes 786440 | tf_op jit(solution)/shard_map/ppermute | solution.py:42
  372.9 12.4 %collective-permute-start.34 = (bf16[64,2048]{1,0:T(8,128)(2,1)}, bf16[64,2048]{1,0:T(8,128)(2,1)S(1)}, u32[]{:S(2)}, u32[]{:S(2)}) collective-permute-start(bf16[64,2048]{1,0:T(8,128)(2,1)} %get-tuple-element.215), channel_id=1, source_target_pairs={{0,16},{8,24},{16,0},{24,8},{1,17},{9,25},{17,1},{25,9},{2,18},{10... | collective-permute-start | bytes 786440 | tf_op jit(solution)/shard_map/ppermute | solution.py:42
  380.9 9.1 %collective-permute-start.35 = (bf16[64,2048]{1,0:T(8,128)(2,1)S(1)}, bf16[64,2048]{1,0:T(8,128)(2,1)S(1)}, u32[]{:S(2)}, u32[]{:S(2)}) collective-permute-start(bf16[64,2048]{1,0:T(8,128)(2,1)S(1)} %copy-done.43), channel_id=1, source_target_pairs={{0,24},{8,16},{16,8},{24,0},{1,25},{9,17},{17,9},{25,1},{2,26},{10... | collective-permute-start | bytes 786440 | tf_op jit(solution)/shard_map/ppermute | solution.py:42
  (45 other events, 918.7 us)
Sparse Core Ops, SparseCore 0:
  80.6 67.3 all-gather.2
  149.5 45.2 all-gather.4
  197.1 59.9 reduce-scatter.2
  286.8 56.1 reduce-scatter.4
